TPU v7x, 32 devices: a whole 2x2x4 slice. The times are simulated.
32 devices in a mesh: grp: 2 (over y), wide: 4 (over z), red: 2 (over x), tok: 2 (over core).
Axes of the slice: x: 2, y: 2, z: 4, core: 2. Of those that a mesh axis runs over, the one named last changes fastest.
Arguments:
- tokens: bfloat16 [1024, 6144], P(('grp', 'tok'), ('red', 'wide')), parts along dimension 0, may hold values from -6 to 6
- ln_gain: bfloat16 [6144], P(('red', 'wide')), may hold values from 0.099609375 to 1.8984375
- q_gain: float32 [4, 128], P('wide'), may hold values from 0.6 to 3
- k_gain: float32 [4, 128], P('wide'), may hold values from 0.6 to 3
- w_qkv: bfloat16 [6144, 4, 384], P(('red', 'tok'), 'wide'), may hold values from -0.078125 to 0.078125
- w_up: bfloat16 [6144, 24576], P(('red', 'tok'), 'wide'), may hold values from -0.078125 to 0.078125
- w_attn: bfloat16 [4, 128, 6144], P('wide', None, ('red', 'tok')), may hold values from -0.25 to 0.25
- w_down: bfloat16 [24576, 6144], P('wide', ('red', 'tok')), may hold values from -0.0546875 to 0.0546875
Outputs:
- block_out: float32 [1024, 6144], P(('grp', 'tok'), ('red', 'wide')), parts along dimension 0
There are 2 independent parts, one for each index of `grp`. A program takes and returns all parts, laid end to end along the dimension named above; an argument that names none is the same for every part. Nothing has to cross between parts.
All inputs are finite; a program needn't handle non-finite values.
Results may differ from a plain program's by a relative error of at most 0.018.
Values may be sent and summed in bfloat16 or wider, within the bound.
No kernel may reach another device: no remote copies, remote signals or barrier semaphores. Data moves between devices by JAX's collectives and lax.ppermute only.
A program may use at most 192 MiB of HBM per device.

v0:
```python
import jax
import jax.numpy as jnp
from jax import lax
from jax.sharding import PartitionSpec as P

D = 6144
PATCHES = 256


EPS = 1e-06


def normalize(values, mean, meansq, gain):
    return (values - mean) * lax.rsqrt(meansq - mean * mean + EPS) * gain.astype(jnp.float32)


def head_norm(values, gain):
    mean = jnp.mean(values, axis=-1, keepdims=True)
    meansq = jnp.mean(values * values, axis=-1, keepdims=True)
    return normalize(values, mean, meansq, gain)


def attend(qkv_part, q_gain, k_gain):
    width = q_gain.shape[1]
    query = head_norm(qkv_part[:, :width], q_gain[0]).astype(jnp.bfloat16)
    key = head_norm(qkv_part[:, width : 2 * width], k_gain[0]).astype(jnp.bfloat16)
    value = qkv_part[:, 2 * width :].astype(jnp.bfloat16)
    quarter = query.shape[0]
    scale = width ** (-0.5)
    own_image = lax.axis_index("red") * quarter // PATCHES
    peak = jnp.full((quarter,), -1e30, jnp.float32)
    key_piece = lax.all_gather(key, "red", axis=0, tiled=True)
    value_piece = lax.all_gather(value, "red", axis=0, tiled=True)
    scores = jnp.dot(query, key_piece.T, preferred_element_type=jnp.float32) * scale
    image_ids = jnp.arange(key_piece.shape[0], dtype=jnp.int32) // PATCHES
    valid = (image_ids == own_image)[None, :]
    masked = jnp.where(valid, scores, -1e30)
    new_peak = jnp.maximum(peak, jnp.max(masked, axis=1))
    weights = jnp.where(valid, jnp.exp(masked - new_peak[:, None]), 0.0)
    total = jnp.sum(weights, axis=1)
    acc = jnp.dot(weights, value_piece.astype(jnp.float32), precision=lax.Precision.HIGHEST)
    peak, total, acc = (new_peak, total, acc)
    return (acc / total[:, None]).astype(jnp.bfloat16)


def body(tokens, ln_gain, q_gain, k_gain, w_qkv, w_up, w_attn, w_down):
    floats = tokens.astype(jnp.float32)
    sums = lax.psum((jnp.sum(floats, axis=1), jnp.sum(floats * floats, axis=1)), ("wide", "red"))
    local = normalize(floats, sums[0][:, None] / D, sums[1][:, None] / D, ln_gain).astype(
        jnp.bfloat16
    )
    normed = lax.all_gather(local, "wide", axis=1, tiled=True)
    qkv_local = w_qkv.reshape(w_qkv.shape[0], w_qkv.shape[1] * w_qkv.shape[2])

    def add_rows(piece):
        return jnp.dot(normed, piece, preferred_element_type=jnp.float32)

    qkv_full = add_rows(lax.all_gather(qkv_local, "tok", axis=0, tiled=True))
    up_full = add_rows(lax.all_gather(w_up, "tok", axis=0, tiled=True))
    qkv_part, up_part = (
        lax.psum_scatter(
            qkv_full.astype(jnp.bfloat16), "red", scatter_dimension=0, tiled=True
        ).astype(jnp.float32),
        lax.psum_scatter(
            up_full.astype(jnp.bfloat16), "red", scatter_dimension=0, tiled=True
        ).astype(jnp.float32),
    )
    attended = attend(qkv_part, q_gain, k_gain)
    hidden = jax.nn.gelu(up_part, approximate=False).astype(jnp.bfloat16)
    attn_cols, down_cols = (
        lax.all_gather(
            w_attn.reshape(w_attn.shape[0] * w_attn.shape[1], w_attn.shape[2]),
            "tok",
            axis=1,
            tiled=True,
        ),
        lax.all_gather(w_down, "tok", axis=1, tiled=True),
    )
    stacked = jnp.concatenate([attn_cols, down_cols], axis=0)
    mixed = jnp.concatenate([attended, hidden], axis=1)
    terms = jnp.dot(
        lax.all_gather(mixed, "red", axis=0, tiled=True),
        stacked,
        preferred_element_type=jnp.float32,
    )
    summed = lax.psum_scatter(
        terms.astype(jnp.bfloat16), "wide", scatter_dimension=1, tiled=True
    ).astype(jnp.float32)
    return floats + summed


def solution(mesh):
    return jax.shard_map(
        body,
        mesh=mesh,
        in_specs=(
            P(("grp", "tok"), ("red", "wide")),
            P(("red", "wide")),
            P("wide", None),
            P("wide", None),
            P(("red", "tok"), "wide", None),
            P(("red", "tok"), "wide"),
            P("wide", None, ("red", "tok")),
            P("wide", ("red", "tok")),
        ),
        out_specs=P(("grp", "tok"), ("red", "wide")),
        check_vma=False,
    )
```

profile of v0, /device:TPU:0, one launch (start us, length us, event | category | flops | bytes accessed | tf_op | source)
XLA Modules:
  0.0 374.2 jit_solution(6396411953561037553)
XLA Ops:
  6.5 1.2 convert_reduce_fusion
  7.8 0.7 convert_element_type.42
  8.4 23.1 %all-reduce = (f32[256]{0:T(256)S(1)}, f32[256]{0:T(256)S(1)}) all-reduce(f32[256]{0:T(256)S(1)} %get-tuple-element.6, f32[256]{0:T(256)S(1)} %get-tuple-element.5), channel_id=1, replica_groups=mesh['grp'=2,'wide'=4,'red'=2,'tok'=2] {'wide','red'}, use_global_device_ids=true, to_apply=%region_3.0 | all-reduce | flops 512 | bytes 4096 | tf_op jit(solution)/shard_map/psum | solution.py:48
  31.5 2.0 fusion.47
  33.6 0.7 all-gather.16.cloned.1.call-update
  34.3 0.7 all-gather.10.cloned.1.call-update
  35.1 33.0 %all-gather.8.cloned.1.call-done = bf16[256,3072]{1,0:T(8,128)(2,1)} async-done(((bf16[256,768]{1,0:T(8,128)(2,1)}), bf16[256,3072]{1,0:T(8,128)(2,1)}) %all-gather.8.cloned.1.call-update) | async-done | bytes 1572880 | tf_op jit(solution)/shard_map/all_gather | solution.py:52
  68.1 11.4 %all-gather.16.cloned.1.call-done = bf16[3072,1,384]{2,0,1:T(8,128)(2,1)} async-done(((bf16[1536,1,384]{2,0,1:T(8,128)(2,1)}), bf16[3072,1,384]{2,0,1:T(8,128)(2,1)}) %all-gather.16.cloned.1.call-update) | async-done | bytes 2359312 | tf_op jit(solution)/shard_map/all_gather | solution.py:58
  79.5 3.8 %fusion.40 = bf16[256,384]{1,0:T(8,128)(2,1)} fusion(bf16[256,3072]{1,0:T(8,128)(2,1)} %all-gather.8.cloned.1.call-done, bf16[3072,1,384]{2,0,1:T(8,128)(2,1)} %all-gather.16.cloned.1.call-done), kind=kOutput, calls=%fused_computation.47 | convolution fusion | flops 604078080 | bytes 4128768 | tf_op jit(solution)/shard_map/dot_general | solution.py:56
  83.3 56.7 %all-gather.10.cloned.1.call-done = bf16[3072,6144]{1,0:T(8,128)(2,1)} async-done(((bf16[1536,6144]{1,0:T(8,128)(2,1)}), bf16[3072,6144]{1,0:T(8,128)(2,1)}) %all-gather.10.cloned.1.call-update) | async-done | bytes 37748752 | tf_op jit(solution)/shard_map/all_gather | solution.py:59
  140.0 18.2 %convolution_convert_fusion = bf16[256,6144]{1,0:T(8,128)(2,1)} fusion(bf16[256,3072]{1,0:T(8,128)(2,1)S(1)} %copy-done.4, bf16[3072,6144]{1,0:T(8,128)(2,1)} %all-gather.10.cloned.1.call-done), kind=kOutput, calls=%fused_computation.4 | convolution fusion | flops 9665249280 | bytes 42467328 | tf_op jit(solution)/shard_map/dot_general | solution.py:56
  159.0 0.9 convert_element_type.45
  159.9 0.8 slice.15
  160.9 4.6 %all_gather.26 = bf16[256,128]{1,0:T(8,128)(2,1)S(1)} all-gather(bf16[128,128]{1,0:T(8,128)(2,1)S(1)} %multiply_convert_fusion), channel_id=1, replica_groups=mesh['grp'=2,'wide'=4,'red'=2,'tok'=2] {'red'}, dimensions={0}, use_global_device_ids=true | all-gather | bytes 98304 | tf_op jit(solution)/shard_map/all_gather | solution.py:32
  165.5 5.3 %all_gather.27 = bf16[256,128]{1,0:T(8,128)(2,1)S(1)} all-gather(bf16[128,128]{1,0:T(8,128)(2,1)S(1)} %slice.15), channel_id=1, replica_groups=mesh['grp'=2,'wide'=4,'red'=2,'tok'=2] {'red'}, dimensions={0}, use_global_device_ids=true | all-gather | bytes 98304 | tf_op jit(solution)/shard_map/all_gather | solution.py:33
  171.6 32.1 %reduce-scatter.6.cloned.1.call-done = bf16[128,6144]{1,0:T(8,128)(2,1)} async-done(((bf16[256,6144]{1,0:T(8,128)(2,1)}), bf16[128,6144]{1,0:T(8,128)(2,1)}) %reduce-scatter.6.cloned.1.call-update) | async-done | bytes 1572880 | tf_op jit(solution)/shard_map/reduce_scatter | solution.py:64
  203.7 7.8 %fusion.8 = bf16[128,6144]{1,0:T(8,128)(2,1)S(1)} fusion(bf16[128,6144]{1,0:T(8,128)(2,1)} %reduce-scatter.6.cloned.1.call-done), kind=kLoop, calls=%fused_computation.10 | loop fusion | flops 51904512 | bytes 3145728 | tf_op jit(solution)/shard_map/convert_element_type | solution.py:69
  211.5 1.3 pad_maximum_fusion
  212.9 2.4 all-gather.1
  215.3 47.7 %all-gather.14.cloned.1.call-done = bf16[6144,3072]{1,0:T(8,128)(2,1)} async-done(((bf16[6144,1536]{1,0:T(8,128)(2,1)}), bf16[6144,3072]{1,0:T(8,128)(2,1)}) %all-gather.14.cloned.1.call-update) | async-done | bytes 37748752 | tf_op jit(solution)/shard_map/all_gather | solution.py:77
  263.0 48.5 %all-gather.12.cloned.1.call-done = bf16[256,6272]{1,0:T(8,128)(2,1)} async-done(((bf16[128,6272]{1,0:T(8,128)(2,1)}), bf16[256,6272]{1,0:T(8,128)(2,1)}) %all-gather.12.cloned.1.call-update) | async-done | bytes 3211280 | tf_op jit(solution)/shard_map/all_gather | solution.py:82
  311.4 18.5 %fusion.4 = bf16[256,3072]{1,0:T(8,128)(2,1)} fusion(bf16[256,6272]{1,0:T(8,128)(2,1)} %all-gather.12.cloned.1.call-done, bf16[6144,3072]{1,0:T(8,128)(2,1)} %all-gather.14.cloned.1.call-done, bf16[128,3072]{1,0:T(8,128)(2,1)S(1)} %bitcast.14), kind=kOutput, calls=%fused_computation.8 | convolution fusion | flops 9942859776 | bytes 43319296 | tf_op jit(solution)/shard_map/dot_general | solution.py:81
  330.0 35.5 %reduce-scatter.8.cloned.1.call-done = bf16[256,768]{1,0:T(8,128)(2,1)} async-done(((bf16[256,3072]{1,0:T(8,128)(2,1)}), bf16[256,768]{1,0:T(8,128)(2,1)}) %reduce-scatter.8.cloned.1.call-update) | async-done | bytes 393232 | tf_op jit(solution)/shard_map/reduce_scatter | solution.py:86
  365.4 2.0 convert_add_fusion
  (35 shorter events, 2.0 us)
Async XLA Ops:
  6.5 61.5 %all-gather.8.cloned.1.call-start = ((), (), s32[]{:S(2)}) async-start(), calls=%async_computation.3 | async-start | bytes 1966080 | tf_op jit(solution)/shard_map/all_gather | solution.py:52
  33.5 45.9 %all-gather.16.cloned.1.call-start = ((), (), s32[]{:S(2)}) async-start(), calls=%async_computation.10 | async-start | bytes 3538944 | tf_op jit(solution)/shard_map/all_gather | solution.py:58
  34.3 105.8 %all-gather.10.cloned.1.call-start = ((), (), s32[]{:S(2)}) async-start(), calls=%async_computation.5 | async-start | bytes 56623104 | tf_op jit(solution)/shard_map/all_gather | solution.py:59
  35.0 124.0 %reduce-scatter.4.cloned.1.call-start = ((), (), s32[]{:S(2)}) async-start(), calls=%async_computation.4 | async-start | bytes 294912 | tf_op jit(solution)/shard_map/reduce_scatter | solution.py:61
  68.1 72.0 %copy-start.4 = (bf16[256,3072]{1,0:T(8,128)(2,1)S(1)}, bf16[256,3072]{1,0:T(8,128)(2,1)}, u32[]{:S(2)}) copy-start(bf16[256,3072]{1,0:T(8,128)(2,1)} %all-gather.8.cloned.1.call-done) | copy-start | bytes 4718596
  83.3 120.4 %reduce-scatter.6.cloned.1.call-start = ((), (), s32[]{:S(2)}) async-start(), calls=%async_computation.6 | async-start | bytes 4718592 | tf_op jit(solution)/shard_map/reduce_scatter | solution.py:64
  158.3 2.5 copy-start.2
  158.3 12.5 %copy-start.3 = (f32[1,128]{1,0:T(1,128)S(1)}, f32[1,128]{1,0:T(1,128)}, u32[]{:S(2)}) copy-start(f32[1,128]{1,0:T(1,128)} %param.10) | copy-start | bytes 1540
  158.3 104.7 %all-gather.14.cloned.1.call-start = ((), (), s32[]{:S(2)}) async-start(), calls=%async_computation.8 | async-start | bytes 56623104 | tf_op jit(solution)/shard_map/all_gather | solution.py:77
  158.9 152.6 %all-gather.12.cloned.1.call-start = ((), (), s32[]{:S(2)}) async-start(), calls=%async_computation.7 | async-start | bytes 4816896 | tf_op jit(solution)/shard_map/all_gather | solution.py:82
  211.5 1.4 copy-start.1
  212.8 152.6 %reduce-scatter.8.cloned.1.call-start = ((), (), s32[]{:S(2)}) async-start(), calls=%async_computation.9 | async-start | bytes 1966080 | tf_op jit(solution)/shard_map/reduce_scatter | solution.py:86
  311.4 54.0 %copy-start = (bf16[256,768]{1,0:T(8,128)(2,1)S(1)}, bf16[256,768]{1,0:T(8,128)(2,1)}, u32[]{:S(2)}) copy-start(bf16[256,768]{1,0:T(8,128)(2,1)} %param.8) | copy-start | bytes 1179652
Sparse Core Ops, SparseCore 0:
  33.7 34.3 all-gather.7
  69.6 9.8 all-gather.15
  81.0 58.9 all-gather.9
  142.1 12.1 reduce-scatter.3
  158.4 45.2 reduce-scatter.5
  205.1 57.7 all-gather.13
  264.6 46.8 all-gather.11
  330.1 35.2 reduce-scatter.7
where the time goes:
time: 375 us; the launch traced here: 374 us
  waiting for transfers between devices  267 us (71%)
  matrix products  41.1 us (11%)
  blocking collectives  35.3 us (9%)
  other arithmetic  16.4 us (4%)
  between operations  13.6 us (4%)
    all_gather x1, waiting for transfers between devices, body(): up_full = add_rows(lax.all_gather(w_up, 'tok', axis=0, tiled=True))  56.7 us
    all_gather x1, waiting for transfers between devices, body(): lax.all_gather(mixed, 'red', axis=0, tiled=True)  48.5 us
    all_gather x1, waiting for transfers between devices, body(): lax.all_gather(w_down, 'tok', axis=1, tiled=True)  47.7 us
    reduce_scatter x1, waiting for transfers between devices, body(): lax.psum_scatter(terms.astype(jnp.bfloat16), 'wide', scatter_dimension=1,...  35.5 us
    all_gather x1, waiting for transfers between devices, body(): normed = lax.all_gather(local, 'wide', axis=1, tiled=True)  33 us
    reduce_scatter x1, waiting for transfers between devices, body(): lax.psum_scatter(up_full.astype(jnp.bfloat16), 'red', scatter_dimension=0...  32.1 us
    psum x1, blocking collectives, body(): lax.psum((jnp.sum(floats, axis=1), jnp.sum(floats * floats, axis=1)), ('w...  23.1 us
    dot_general x2, matrix products, add_rows(): return jnp.dot(normed, piece, preferred_element_type=jnp.float32)  22 us
  transfers between devices with their start and end apart: 8, of which 7 were waited for; matrix products, arithmetic and copies ran while one was open for 9% of the time, Pallas kernels for 0%

commit v1 on v0

v1 whole, which is shorter than its diff:
```python
import jax
import jax.numpy as jnp
from jax import lax
from jax.sharding import PartitionSpec as P

D = 6144
PATCHES = 256
EPS = 1e-06
CHUNKS = 2
PIECES = 2


def normalize(values, mean, meansq, gain):
    return (values - mean) * lax.rsqrt(meansq - mean * mean + EPS) * gain.astype(jnp.float32)


def head_norm(values, gain):
    mean = jnp.mean(values, axis=-1, keepdims=True)
    meansq = jnp.mean(values * values, axis=-1, keepdims=True)
    return normalize(values, mean, meansq, gain)


def attend(qkv, q_gain, k_gain):
    width = q_gain.shape[1]
    query = head_norm(qkv[:, :width], q_gain[0]).astype(jnp.bfloat16)
    key = head_norm(qkv[:, width : 2 * width], k_gain[0]).astype(jnp.bfloat16)
    value = qkv[:, 2 * width :].astype(jnp.bfloat16)
    query, key, value = (a.reshape(-1, PATCHES, width) for a in (query, key, value))
    scores = jnp.einsum("ipd,iqd->ipq", query, key, preferred_element_type=jnp.float32)
    scores = scores * width ** (-0.5)
    weights = jnp.exp(scores - jnp.max(scores, axis=-1, keepdims=True))
    total = jnp.sum(weights, axis=-1, keepdims=True)
    acc = jnp.einsum(
        "ipq,iqd->ipd", weights, value.astype(jnp.float32), precision=lax.Precision.HIGHEST
    )
    return (acc / total).astype(jnp.bfloat16).reshape(-1, width)


def make_body(mesh):
    n_red = mesh.shape["red"]

    def swap(x):
        return lax.ppermute(x, "tok", [(0, 1), (1, 0)])

    def sum_red(x):
        total = x.astype(jnp.float32)
        for shift in range(1, n_red):
            pairs = [(i, (i + shift) % n_red) for i in range(n_red)]
            total = total + lax.ppermute(x, "red", pairs).astype(jnp.float32)
        return total

    def body(tokens, ln_gain, q_gain, k_gain, w_qkv, w_up, w_attn, w_down):
        core = lax.axis_index("tok")
        rows = tokens.shape[0] // CHUNKS
        qkv_rows = w_qkv.reshape(w_qkv.shape[0], w_qkv.shape[1] * w_qkv.shape[2])
        attn_rows = w_attn.reshape(w_attn.shape[0] * w_attn.shape[1], w_attn.shape[2])
        depth = w_up.shape[0]
        piece = w_up.shape[1] // PIECES
        gain = lax.all_gather(ln_gain, "wide", axis=0, tiled=True)

        inputs = []
        ups = []
        for c in range(CHUNKS):
            raw = lax.all_gather(
                tokens[c * rows : (c + 1) * rows], "wide", axis=1, tiled=True
            ).astype(jnp.float32)
            sums = sum_red(jnp.stack([jnp.sum(raw, axis=1), jnp.sum(raw * raw, axis=1)]))
            normed = normalize(raw, sums[0][:, None] / D, sums[1][:, None] / D, gain)
            normed = normed.astype(jnp.bfloat16)
            mine = lax.dynamic_slice_in_dim(normed, core * depth, depth, axis=1)
            theirs = lax.dynamic_slice_in_dim(normed, (1 - core) * depth, depth, axis=1)
            inputs.append(jnp.concatenate([mine, swap(theirs)], axis=0))

        def project(x, weight):
            half = x.shape[0] // 2
            part = jnp.dot(x, weight, preferred_element_type=jnp.float32)
            other = swap(part[half:].astype(jnp.bfloat16)).astype(jnp.float32)
            return sum_red((part[:half] + other).astype(jnp.bfloat16))

        for c in range(CHUNKS):
            ups.append(
                [
                    project(inputs[c], w_up[:, p * piece : (p + 1) * piece])
                    for p in range(PIECES)
                ]
            )
        qkv = jnp.concatenate([project(x, qkv_rows) for x in inputs], axis=0)
        attended = attend(qkv, q_gain, k_gain)
        attended_other = swap(attended)

        outs = []
        for c in range(CHUNKS):
            pick = slice(c * rows, (c + 1) * rows)
            both = jnp.concatenate([attended[pick], attended_other[pick]], axis=0)
            terms = jnp.dot(both, attn_rows, preferred_element_type=jnp.float32)
            for p in range(PIECES):
                hidden = jax.nn.gelu(ups[c][p], approximate=False).astype(jnp.bfloat16)
                both = jnp.concatenate([hidden, swap(hidden)], axis=0)
                terms = terms + jnp.dot(
                    both,
                    w_down[p * piece : (p + 1) * piece],
                    preferred_element_type=jnp.float32,
                )
            terms = terms.astype(jnp.bfloat16)
            kept, got = terms[:rows], swap(terms[rows:])
            lower = jnp.where(core == 0, kept, got)
            upper = jnp.where(core == 0, got, kept)
            summed = lax.psum_scatter(
                jnp.concatenate([lower, upper], axis=1), "wide", scatter_dimension=1, tiled=True
            ).astype(jnp.float32)
            outs.append(tokens[pick].astype(jnp.float32) + summed)
        return jnp.concatenate(outs, axis=0)

    return body


def solution(mesh):
    return jax.shard_map(
        make_body(mesh),
        mesh=mesh,
        in_specs=(
            P(("grp", "tok"), ("red", "wide")),
            P(("red", "wide")),
            P("wide", None),
            P("wide", None),
            P(("red", "tok"), "wide", None),
            P(("red", "tok"), "wide"),
            P("wide", None, ("red", "tok")),
            P("wide", ("red", "tok")),
        ),
        out_specs=P(("grp", "tok"), ("red", "wide")),
        check_vma=False,
    )
```

time: 375 us -> 255 us (0.68)
  waiting for transfers between devices: 267 us -> 109 us
  blocking collectives: 35.3 us -> 51.7 us
  starting transfers between devices: 0.28 us -> 13.3 us
  other arithmetic: 16.4 us -> 20.5 us
    all_gather x5 -> x0, waiting for transfers between devices: 197 us -> none  [the longest x1 56.7 us: body(): up_full = add_rows(lax.all_gather(w_up, 'tok', axis=0, tiled=True))]
    ppermute x0 -> x23, waiting for transfers between devices: none -> 64.8 us  [the longest x8 61.7 us: sum_red(): total = total + lax.ppermute(x, 'red', pairs).astype(jnp.float32)]
    all_gather x3, blocking collectives: 12.2 us -> 51.7 us  [the longest x2 38.6 us: body(): lax.all_gather(tokens[c * rows:(c + 1) * rows], 'wide', axis=1, tiled=True)]
    reduce_scatter x3 -> x2, waiting for transfers between devices: 67.6 us -> 44.2 us  [body(): lax.psum_scatter(jnp.concatenate([lower, upper], axis=1), 'wide', scatter...]
    psum x1 -> x0, blocking collectives: 23.1 us -> none  [body(): lax.psum((jnp.sum(floats, axis=1), jnp.sum(floats * floats, axis=1)), ('w...]
    ppermute x0 -> x23, starting transfers between devices: none -> 13.2 us  [the longest x8 9.22 us: sum_red(): total = total + lax.ppermute(x, 'red', pairs).astype(jnp.float32)]
    convert_element_type x4 -> x11, other arithmetic: 10.8 us -> 15.4 us  [the longest x4 14 us: body(): hidden = jax.nn.gelu(ups[c][p], approximate=False).astype(jnp.bfloat16)]
    dot_general x5 -> x14, matrix products: 41.1 us -> 42.8 us  [the longest x6 21.9 us: project(): part = jnp.dot(x, weight, preferred_element_type=jnp.float32)]
  transfers between devices with their start and end apart: 8 -> 25, of which waited for: 7 -> 11; matrix products, arithmetic and copies ran while one was open for 9% -> 24% of each run, Pallas kernels for 0% -> 0%
where the time goes in v1:
time: 255 us
  waiting for transfers between devices  109 us (43%)
  blocking collectives  51.7 us (20%)
  matrix products  42.8 us (17%)
  other arithmetic  20.5 us (8%)
  between operations  14 us (5%)
  starting transfers between devices  13.3 us (5%)
  local copies, waits for them, and re-layouts  3.33 us (1%)
    ppermute x8, waiting for transfers between devices, sum_red(): total = total + lax.ppermute(x, 'red', pairs).astype(jnp.float32)  61.7 us
    reduce_scatter x2, waiting for transfers between devices, body(): lax.psum_scatter(jnp.concatenate([lower, upper], axis=1), 'wide', scatter...  44.2 us
    all_gather x2, blocking collectives, body(): lax.all_gather(tokens[c * rows:(c + 1) * rows], 'wide', axis=1, tiled=True)  38.6 us
    dot_general x6, matrix products, project(): part = jnp.dot(x, weight, preferred_element_type=jnp.float32)  21.9 us
    dot_general x4, matrix products, body(): jnp.dot(both, w_down[p * piece:(p + 1) * piece], preferred_element_type=j...  18.7 us
    convert_element_type x4, other arithmetic, body(): hidden = jax.nn.gelu(ups[c][p], approximate=False).astype(jnp.bfloat16)  14 us
    all_gather x1, blocking collectives, body(): gain = lax.all_gather(ln_gain, 'wide', axis=0, tiled=True)  13 us
    ppermute x8, starting transfers between devices, sum_red(): total = total + lax.ppermute(x, 'red', pairs).astype(jnp.float32)  9.22 us
  transfers between devices with their start and end apart: 25, of which 11 were waited for; matrix products, arithmetic and copies ran while one was open for 24% of the time, Pallas kernels for 0%

profile of v1, /device:TPU:0, one launch (start us, length us, event | category | flops | bytes accessed | tf_op | source)
XLA Modules:
  0.0 254.6 jit_solution(3818327137480423027)
XLA Ops:
  7.7 21.3 %all_gather.9 = bf16[128,3072]{1,0:T(8,128)(2,1)S(1)} all-gather(bf16[128,768]{1,0:T(8,128)(2,1)S(1)} %get-tuple-element.28), channel_id=1, replica_groups=mesh['grp'=2,'wide'=4,'red'=2,'tok'=2] {'wide'}, dimensions={1}, use_global_device_ids=true | all-gather | bytes 983040 | tf_op jit(solution)/shard_map/all_gather | solution.py:64
  29.3 1.6 collective-permute-start
  30.9 17.3 %all_gather.11 = bf16[128,3072]{1,0:T(8,128)(2,1)S(1)} all-gather(bf16[128,768]{1,0:T(8,128)(2,1)S(1)} %get-tuple-element.29), channel_id=1, replica_groups=mesh['grp'=2,'wide'=4,'red'=2,'tok'=2] {'wide'}, dimensions={1}, use_global_device_ids=true | all-gather | bytes 983040 | tf_op jit(solution)/shard_map/all_gather | solution.py:64
  49.4 13.0 %all-gather = bf16[4,1,768]{2,1,0:T(2,128)(2,1)S(1)} all-gather(bf16[1,1,768]{2,1,0:T(2,128)(2,1)S(1)} %reshape.135), channel_id=1, replica_groups=mesh['grp'=2,'wide'=4,'red'=2,'tok'=2] {'wide'}, dimensions={0}, use_global_device_ids=true | all-gather | bytes 7680 | tf_op jit(solution)/shard_map/all_gather | solution.py:59
  67.0 5.2 %fusion.12 = f32[256,3072]{1,0:T(8,128)S(1)} fusion(bf16[1536,6144]{1,0:T(8,128)(2,1)} %param.13, bf16[128,1536]{1,0:T(8,128)(2,1)S(1)} %collective-permute-done.5, bf16[128,1536]{1,0:T(8,128)(2,1)S(1)} %get-tuple-element.21), kind=kOutput, calls=%fused_computation.12 | convolution fusion | flops 2417491968 | bytes 13369344 | tf_op jit(solution)/shard_map/dot_general | solution.py:76
  72.5 5.2 %fusion.4 = f32[256,3072]{1,0:T(8,128)S(1)} fusion(bf16[1536,6144]{1,0:T(8,128)(2,1)} %param.13, bf16[128,1536]{1,0:T(8,128)(2,1)S(1)} %collective-permute-done.5, bf16[128,1536]{1,0:T(8,128)(2,1)S(1)} %get-tuple-element.21), kind=kOutput, calls=%fused_computation.4 | convolution fusion | flops 2417491968 | bytes 13369344 | tf_op jit(solution)/shard_map/dot_general | solution.py:76
  78.2 5.2 %fusion.14 = f32[256,3072]{1,0:T(8,128)S(1)} fusion(bf16[1536,6144]{1,0:T(8,128)(2,1)} %param.13, bf16[128,1536]{1,0:T(8,128)(2,1)S(1)} %collective-permute-done.1, bf16[128,1536]{1,0:T(8,128)(2,1)S(1)} %get-tuple-element.19), kind=kOutput, calls=%fused_computation.14 | convolution fusion | flops 2417491968 | bytes 13369344 | tf_op jit(solution)/shard_map/dot_general | solution.py:76
  83.7 5.2 %fusion.6 = f32[256,3072]{1,0:T(8,128)S(1)} fusion(bf16[1536,6144]{1,0:T(8,128)(2,1)} %param.13, bf16[128,1536]{1,0:T(8,128)(2,1)S(1)} %collective-permute-done.1, bf16[128,1536]{1,0:T(8,128)(2,1)S(1)} %get-tuple-element.19), kind=kOutput, calls=%fused_computation.6 | convolution fusion | flops 2417491968 | bytes 13369344 | tf_op jit(solution)/shard_map/dot_general | solution.py:76
  90.7 3.7 %collective-permute-done.3 = bf16[128,384]{1,0:T(8,128)(2,1)S(1)} collective-permute-done((bf16[128,384]{1,0:T(8,128)(2,1)S(1)}, bf16[128,384]{1,0:T(8,128)(2,1)S(1)}, u32[]{:S(2)}, u32[]{:S(2)}) %collective-permute-start.3) | collective-permute-done | bytes 98336 | tf_op jit(solution)/shard_map/ppermute | solution.py:49
  95.7 3.4 %collective-permute-done.7 = bf16[128,384]{1,0:T(8,128)(2,1)S(1)} collective-permute-done((bf16[128,384]{1,0:T(8,128)(2,1)S(1)}, bf16[128,384]{1,0:T(8,128)(2,1)S(1)}, u32[]{:S(2)}, u32[]{:S(2)}) %collective-permute-start.7) | collective-permute-done | bytes 98336 | tf_op jit(solution)/shard_map/ppermute | solution.py:49
  107.1 15.6 %collective-permute-done.17 = bf16[128,3072]{1,0:T(8,128)(2,1)S(1)} collective-permute-done((bf16[128,3072]{1,0:T(8,128)(2,1)S(1)}, bf16[128,3072]{1,0:T(8,128)(2,1)S(1)}, u32[]{:S(2)}, u32[]{:S(2)}) %collective-permute-start.17) | collective-permute-done | bytes 786464 | tf_op jit(solution)/shard_map/ppermute | solution.py:49
  122.7 3.5 %fusion.36 = bf16[128,3072]{1,0:T(8,128)(2,1)S(1)} fusion(bf16[128,3072]{1,0:T(8,128)(2,1)S(1)} %collective-permute-done.17, bf16[128,3072]{1,0:T(8,128)(2,1)S(1)} %fusion.41), kind=kLoop, calls=%fused_computation.48 | loop fusion | flops 26738688 | bytes 2359296 | tf_op jit(solution)/shard_map/convert_element_type | solution.py:97
  126.3 13.3 %collective-permute-done.20 = bf16[128,3072]{1,0:T(8,128)(2,1)S(1)} collective-permute-done((bf16[128,3072]{1,0:T(8,128)(2,1)S(1)}, bf16[128,3072]{1,0:T(8,128)(2,1)S(1)}, u32[]{:S(2)}, u32[]{:S(2)}) %collective-permute-start.20) | collective-permute-done | bytes 786464 | tf_op jit(solution)/shard_map/ppermute | solution.py:49
  139.6 3.5 %fusion.39 = bf16[128,3072]{1,0:T(8,128)(2,1)S(1)} fusion(bf16[128,3072]{1,0:T(8,128)(2,1)S(1)} %collective-permute-done.20, bf16[128,3072]{1,0:T(8,128)(2,1)S(1)} %fusion.40), kind=kLoop, calls=%fused_computation.51 | loop fusion | flops 26738688 | bytes 2359296 | tf_op jit(solution)/shard_map/convert_element_type | solution.py:97
  143.2 13.3 %collective-permute-done.10 = bf16[128,3072]{1,0:T(8,128)(2,1)S(1)} collective-permute-done((bf16[128,3072]{1,0:T(8,128)(2,1)S(1)}, bf16[128,3072]{1,0:T(8,128)(2,1)S(1)}, u32[]{:S(2)}, u32[]{:S(2)}) %collective-permute-start.10) | collective-permute-done | bytes 786464 | tf_op jit(solution)/shard_map/ppermute | solution.py:49
  156.4 3.5 %fusion.30 = bf16[128,3072]{1,0:T(8,128)(2,1)S(1)} fusion(bf16[128,3072]{1,0:T(8,128)(2,1)S(1)} %collective-permute-done.10, bf16[128,3072]{1,0:T(8,128)(2,1)S(1)} %fusion.43), kind=kLoop, calls=%fused_computation.42 | loop fusion | flops 26738688 | bytes 2359296 | tf_op jit(solution)/shard_map/convert_element_type | solution.py:97
  160.0 12.5 %collective-permute-done.13 = bf16[128,3072]{1,0:T(8,128)(2,1)S(1)} collective-permute-done((bf16[128,3072]{1,0:T(8,128)(2,1)S(1)}, bf16[128,3072]{1,0:T(8,128)(2,1)S(1)}, u32[]{:S(2)}, u32[]{:S(2)}) %collective-permute-start.13) | collective-permute-done | bytes 786464 | tf_op jit(solution)/shard_map/ppermute | solution.py:49
  172.5 3.5 %fusion.33 = bf16[128,3072]{1,0:T(8,128)(2,1)S(1)} fusion(bf16[128,3072]{1,0:T(8,128)(2,1)S(1)} %collective-permute-done.13, bf16[128,3072]{1,0:T(8,128)(2,1)S(1)} %fusion.42), kind=kLoop, calls=%fused_computation.45 | loop fusion | flops 26738688 | bytes 2359296 | tf_op jit(solution)/shard_map/convert_element_type | solution.py:97
  176.1 5.2 %fusion.8 = f32[256,1536]{1,0:T(8,128)S(1)} fusion(bf16[6144,1536]{1,0:T(8,128)(2,1)} %param.15, bf16[128,3072]{1,0:T(8,128)(2,1)S(1)} %collective-permute-done.18, bf16[128,3072]{1,0:T(8,128)(2,1)S(1)} %fusion.36), kind=kOutput, calls=%fused_computation.8 | convolution fusion | flops 2419064832 | bytes 12582912 | tf_op jit(solution)/shard_map/dot_general | solution.py:99
  181.4 5.4 %fusion = f32[256,1536]{1,0:T(8,128)S(1)} fusion(bf16[6144,1536]{1,0:T(8,128)(2,1)} %param.15, bf16[128,3072]{1,0:T(8,128)(2,1)S(1)} %collective-permute-done.21, bf16[128,3072]{1,0:T(8,128)(2,1)S(1)} %fusion.39), kind=kOutput, calls=%fused_computation | convolution fusion | flops 2419064832 | bytes 12582912 | tf_op jit(solution)/shard_map/dot_general | solution.py:99
  187.8 5.5 %fusion.10 = f32[256,1536]{1,0:T(8,128)S(1)} fusion(bf16[6144,1536]{1,0:T(8,128)(2,1)} %param.15, bf16[128,3072]{1,0:T(8,128)(2,1)S(1)} %collective-permute-done.11, bf16[128,3072]{1,0:T(8,128)(2,1)S(1)} %fusion.30), kind=kOutput, calls=%fused_computation.10 | convolution fusion | flops 2419064832 | bytes 12582912 | tf_op jit(solution)/shard_map/dot_general | solution.py:99
  193.7 2.6 %fusion.2 = f32[256,1536]{1,0:T(8,128)S(1)} fusion(bf16[6144,1536]{1,0:T(8,128)(2,1)S(1)} %bitcast.55, bf16[128,3072]{1,0:T(8,128)(2,1)S(1)} %collective-permute-done.14, bf16[128,3072]{1,0:T(8,128)(2,1)S(1)} %fusion.33), kind=kOutput, calls=%fused_computation.2 | convolution fusion | flops 2419064832 | bytes 12582912 | tf_op jit(solution)/shard_map/dot_general | solution.py:99
  201.5 19.3 %reduce-scatter.5.cloned.1.call-done = bf16[128,768]{1,0:T(8,128)(2,1)} async-done(((bf16[128,3072]{1,0:T(8,128)(2,1)}), bf16[128,768]{1,0:T(8,128)(2,1)}) %reduce-scatter.5.cloned.1.call-update) | async-done | bytes 196624 | tf_op jit(solution)/shard_map/reduce_scatter | solution.py:108
  220.8 24.9 %reduce-scatter.3.cloned.1.call-done = bf16[128,768]{1,0:T(8,128)(2,1)} async-done(((bf16[128,3072]{1,0:T(8,128)(2,1)}), bf16[128,768]{1,0:T(8,128)(2,1)}) %reduce-scatter.3.cloned.1.call-update) | async-done | bytes 196624 | tf_op jit(solution)/shard_map/reduce_scatter | solution.py:108
  (117 shorter events, 28.0 us)
Async XLA Ops:
  6.5 214.3 %reduce-scatter.5.cloned.1.call-start = ((), (), s32[]{:S(2)}) async-start(), calls=%async_computation.3 | async-start | bytes 983040 | tf_op jit(solution)/shard_map/reduce_scatter | solution.py:108
  29.3 33.2 %collective-permute-start = (f32[2,128]{1,0:T(2,128)S(1)}, f32[2,128]{1,0:T(2,128)S(1)}, u32[]{:S(2)}, u32[]{:S(2)}) collective-permute-start(f32[2,128]{1,0:T(2,128)S(1)} %pad_maximum_fusion.12), channel_id=1, source_target_pairs={{0,2},{2,0},{1,3},{3,1},{4,6},{6,4},{5,7},{7,5},{8,10},{10,8},{9,1... | collective-permute-start | bytes 3080 | tf_op jit(solution)/shard_map/ppermute | solution.py:49
  48.5 14.0 %collective-permute-start.4 = (f32[2,128]{1,0:T(2,128)S(1)}, f32[2,128]{1,0:T(2,128)S(1)}, u32[]{:S(2)}, u32[]{:S(2)}) collective-permute-start(f32[2,128]{1,0:T(2,128)S(1)} %pad_maximum_fusion.13), channel_id=1, source_target_pairs={{0,2},{2,0},{1,3},{3,1},{4,6},{6,4},{5,7},{7,5},{8,10},{10,8},{9,1... | collective-permute-start | bytes 3080 | tf_op jit(solution)/shard_map/ppermute | solution.py:49
  63.3 1.8 collective-permute-start.1
  63.5 2.4 collective-permute-start.5
  65.7 23.3 %collective-permute-start.2 = (bf16[128,384]{1,0:T(8,128)(2,1)S(1)}, bf16[128,384]{1,0:T(8,128)(2,1)S(1)}, u32[]{:S(2)}, u32[]{:S(2)}) collective-permute-start(bf16[128,384]{1,0:T(8,128)(2,1)S(1)} %slice.250), channel_id=1, source_target_pairs={{0,1},{1,0},{2,3},{3,2},{4,5},{5,4},{6,7},{7,6},{8,9},{9,8},{10,11... | collective-permute-start | bytes 294920 | tf_op jit(solution)/shard_map/ppermute | solution.py:43
  66.5 22.9 %collective-permute-start.6 = (bf16[128,384]{1,0:T(8,128)(2,1)S(1)}, bf16[128,384]{1,0:T(8,128)(2,1)S(1)}, u32[]{:S(2)}, u32[]{:S(2)}) collective-permute-start(bf16[128,384]{1,0:T(8,128)(2,1)S(1)} %slice.249), channel_id=1, source_target_pairs={{0,1},{1,0},{2,3},{3,2},{4,5},{5,4},{6,7},{7,6},{8,9},{9,8},{10,11... | collective-permute-start | bytes 294920 | tf_op jit(solution)/shard_map/ppermute | solution.py:43
  72.2 29.9 %collective-permute-start.16 = (bf16[128,3072]{1,0:T(8,128)(2,1)S(1)}, bf16[128,3072]{1,0:T(8,128)(2,1)S(1)}, u32[]{:S(2)}, u32[]{:S(2)}) collective-permute-start(bf16[128,3072]{1,0:T(8,128)(2,1)S(1)} %slice.246), channel_id=1, source_target_pairs={{0,1},{1,0},{2,3},{3,2},{4,5},{5,4},{6,7},{7,6},{8,9},{9,8},{10,11... | collective-permute-start | bytes 2359304 | tf_op jit(solution)/shard_map/ppermute | solution.py:43
  77.8 25.7 %collective-permute-start.19 = (bf16[128,3072]{1,0:T(8,128)(2,1)S(1)}, bf16[128,3072]{1,0:T(8,128)(2,1)S(1)}, u32[]{:S(2)}, u32[]{:S(2)}) collective-permute-start(bf16[128,3072]{1,0:T(8,128)(2,1)S(1)} %slice.245), channel_id=1, source_target_pairs={{0,1},{1,0},{2,3},{3,2},{4,5},{5,4},{6,7},{7,6},{8,9},{9,8},{10,11... | collective-permute-start | bytes 2359304 | tf_op jit(solution)/shard_map/ppermute | solution.py:43
  83.5 21.1 %collective-permute-start.9 = (bf16[128,3072]{1,0:T(8,128)(2,1)S(1)}, bf16[128,3072]{1,0:T(8,128)(2,1)S(1)}, u32[]{:S(2)}, u32[]{:S(2)}) collective-permute-start(bf16[128,3072]{1,0:T(8,128)(2,1)S(1)} %slice.248), channel_id=1, source_target_pairs={{0,1},{1,0},{2,3},{3,2},{4,5},{5,4},{6,7},{7,6},{8,9},{9,8},{10,11... | collective-permute-start | bytes 2359304 | tf_op jit(solution)/shard_map/ppermute | solution.py:43
  89.1 17.0 %collective-permute-start.12 = (bf16[128,3072]{1,0:T(8,128)(2,1)S(1)}, bf16[128,3072]{1,0:T(8,128)(2,1)S(1)}, u32[]{:S(2)}, u32[]{:S(2)}) collective-permute-start(bf16[128,3072]{1,0:T(8,128)(2,1)S(1)} %slice.247), channel_id=1, source_target_pairs={{0,1},{1,0},{2,3},{3,2},{4,5},{5,4},{6,7},{7,6},{8,9},{9,8},{10,11... | collective-permute-start | bytes 2359304 | tf_op jit(solution)/shard_map/ppermute | solution.py:43
  89.5 5.0 %collective-permute-start.3 = (bf16[128,384]{1,0:T(8,128)(2,1)S(1)}, bf16[128,384]{1,0:T(8,128)(2,1)S(1)}, u32[]{:S(2)}, u32[]{:S(2)}) collective-permute-start(bf16[128,384]{1,0:T(8,128)(2,1)S(1)} %fusion.93), channel_id=1, source_target_pairs={{0,2},{2,0},{1,3},{3,1},{4,6},{6,4},{5,7},{7,5},{8,10},{10,8},{9,1... | collective-permute-start | bytes 294920 | tf_op jit(solution)/shard_map/ppermute | solution.py:49
  94.4 4.6 %collective-permute-start.7 = (bf16[128,384]{1,0:T(8,128)(2,1)S(1)}, bf16[128,384]{1,0:T(8,128)(2,1)S(1)}, u32[]{:S(2)}, u32[]{:S(2)}) collective-permute-start(bf16[128,384]{1,0:T(8,128)(2,1)S(1)} %fusion.92), channel_id=1, source_target_pairs={{0,2},{2,0},{1,3},{3,1},{4,6},{6,4},{5,7},{7,5},{8,10},{10,8},{9,1... | collective-permute-start | bytes 294920 | tf_op jit(solution)/shard_map/ppermute | solution.py:49
  102.3 20.5 %collective-permute-start.17 = (bf16[128,3072]{1,0:T(8,128)(2,1)S(1)}, bf16[128,3072]{1,0:T(8,128)(2,1)S(1)}, u32[]{:S(2)}, u32[]{:S(2)}) collective-permute-start(bf16[128,3072]{1,0:T(8,128)(2,1)S(1)} %fusion.41), channel_id=1, source_target_pairs={{0,2},{2,0},{1,3},{3,1},{4,6},{6,4},{5,7},{7,5},{8,10},{10,8},{9,1... | collective-permute-start | bytes 2359304 | tf_op jit(solution)/shard_map/ppermute | solution.py:49
  103.7 35.9 %collective-permute-start.20 = (bf16[128,3072]{1,0:T(8,128)(2,1)S(1)}, bf16[128,3072]{1,0:T(8,128)(2,1)S(1)}, u32[]{:S(2)}, u32[]{:S(2)}) collective-permute-start(bf16[128,3072]{1,0:T(8,128)(2,1)S(1)} %fusion.40), channel_id=1, source_target_pairs={{0,2},{2,0},{1,3},{3,1},{4,6},{6,4},{5,7},{7,5},{8,10},{10,8},{9,1... | collective-permute-start | bytes 2359304 | tf_op jit(solution)/shard_map/ppermute | solution.py:49
  104.8 51.7 %collective-permute-start.10 = (bf16[128,3072]{1,0:T(8,128)(2,1)S(1)}, bf16[128,3072]{1,0:T(8,128)(2,1)S(1)}, u32[]{:S(2)}, u32[]{:S(2)}) collective-permute-start(bf16[128,3072]{1,0:T(8,128)(2,1)S(1)} %fusion.43), channel_id=1, source_target_pairs={{0,2},{2,0},{1,3},{3,1},{4,6},{6,4},{5,7},{7,5},{8,10},{10,8},{9,1... | collective-permute-start | bytes 2359304 | tf_op jit(solution)/shard_map/ppermute | solution.py:49
  106.2 66.3 %collective-permute-start.13 = (bf16[128,3072]{1,0:T(8,128)(2,1)S(1)}, bf16[128,3072]{1,0:T(8,128)(2,1)S(1)}, u32[]{:S(2)}, u32[]{:S(2)}) collective-permute-start(bf16[128,3072]{1,0:T(8,128)(2,1)S(1)} %fusion.42), channel_id=1, source_target_pairs={{0,2},{2,0},{1,3},{3,1},{4,6},{6,4},{5,7},{7,5},{8,10},{10,8},{9,1... | collective-permute-start | bytes 2359304 | tf_op jit(solution)/shard_map/ppermute | solution.py:49
  126.2 49.9 %collective-permute-start.18 = (bf16[128,3072]{1,0:T(8,128)(2,1)S(1)}, bf16[128,3072]{1,0:T(8,128)(2,1)S(1)}, u32[]{:S(2)}, u32[]{:S(2)}) collective-permute-start(bf16[128,3072]{1,0:T(8,128)(2,1)S(1)} %fusion.36), channel_id=1, source_target_pairs={{0,1},{1,0},{2,3},{3,2},{4,5},{5,4},{6,7},{7,6},{8,9},{9,8},{10,11... | collective-permute-start | bytes 2359304 | tf_op jit(solution)/shard_map/ppermute | solution.py:43
  143.1 38.3 %collective-permute-start.21 = (bf16[128,3072]{1,0:T(8,128)(2,1)S(1)}, bf16[128,3072]{1,0:T(8,128)(2,1)S(1)}, u32[]{:S(2)}, u32[]{:S(2)}) collective-permute-start(bf16[128,3072]{1,0:T(8,128)(2,1)S(1)} %fusion.39), channel_id=1, source_target_pairs={{0,1},{1,0},{2,3},{3,2},{4,5},{5,4},{6,7},{7,6},{8,9},{9,8},{10,11... | collective-permute-start | bytes 2359304 | tf_op jit(solution)/shard_map/ppermute | solution.py:43
  159.9 27.8 %collective-permute-start.11 = (bf16[128,3072]{1,0:T(8,128)(2,1)S(1)}, bf16[128,3072]{1,0:T(8,128)(2,1)S(1)}, u32[]{:S(2)}, u32[]{:S(2)}) collective-permute-start(bf16[128,3072]{1,0:T(8,128)(2,1)S(1)} %fusion.30), channel_id=1, source_target_pairs={{0,1},{1,0},{2,3},{3,2},{4,5},{5,4},{6,7},{7,6},{8,9},{9,8},{10,11... | collective-permute-start | bytes 2359304 | tf_op jit(solution)/shard_map/ppermute | solution.py:43
  176.0 17.3 %collective-permute-start.14 = (bf16[128,3072]{1,0:T(8,128)(2,1)S(1)}, bf16[128,3072]{1,0:T(8,128)(2,1)S(1)}, u32[]{:S(2)}, u32[]{:S(2)}) collective-permute-start(bf16[128,3072]{1,0:T(8,128)(2,1)S(1)} %fusion.33), channel_id=1, source_target_pairs={{0,1},{1,0},{2,3},{3,2},{4,5},{5,4},{6,7},{7,6},{8,9},{9,8},{10,11... | collective-permute-start | bytes 2359304 | tf_op jit(solution)/shard_map/ppermute | solution.py:43
  187.2 9.0 %collective-permute-start.22 = (bf16[128,1536]{1,0:T(8,128)(2,1)S(1)}, bf16[128,1536]{1,0:T(8,128)(2,1)S(1)}, u32[]{:S(2)}, u32[]{:S(2)}) collective-permute-start(bf16[128,1536]{1,0:T(8,128)(2,1)S(1)} %slice.176), channel_id=1, source_target_pairs={{0,1},{1,0},{2,3},{3,2},{4,5},{5,4},{6,7},{7,6},{8,9},{9,8},{10,11... | collective-permute-start | bytes 1179656 | tf_op jit(solution)/shard_map/ppermute | solution.py:43
  197.3 48.4 %reduce-scatter.3.cloned.1.call-start = ((), (), s32[]{:S(2)}) async-start(), calls=%async_computation.2 | async-start | bytes 983040 | tf_op jit(solution)/shard_map/reduce_scatter | solution.py:108
  198.5 1.9 collective-permute-start.15
  (13 other events, 267.7 us)
Sparse Core Ops, SparseCore 0:
  197.4 23.3 reduce-scatter.4
  223.1 22.5 reduce-scatter.2

commit v2 on v1

v2 whole, which is shorter than its diff:
```python
import jax
import jax.numpy as jnp
from jax import lax
from jax.sharding import PartitionSpec as P

D = 6144
PATCHES = 256
EPS = 1e-06
SHARES = (1, 2, 1)
PIECES = 2


def normalize(values, mean, meansq, gain):
    return (values - mean) * lax.rsqrt(meansq - mean * mean + EPS) * gain.astype(jnp.float32)


def head_norm(values, gain):
    mean = jnp.mean(values, axis=-1, keepdims=True)
    meansq = jnp.mean(values * values, axis=-1, keepdims=True)
    return normalize(values, mean, meansq, gain)


def attend(qkv, q_gain, k_gain):
    width = q_gain.shape[1]
    query = head_norm(qkv[:, :width], q_gain[0]).astype(jnp.bfloat16)
    key = head_norm(qkv[:, width : 2 * width], k_gain[0]).astype(jnp.bfloat16)
    value = qkv[:, 2 * width :].astype(jnp.bfloat16)
    query, key, value = (a.reshape(-1, PATCHES, width) for a in (query, key, value))
    scores = jnp.einsum("ipd,iqd->ipq", query, key, preferred_element_type=jnp.float32)
    scores = scores * width ** (-0.5)
    weights = jnp.exp(scores - jnp.max(scores, axis=-1, keepdims=True))
    total = jnp.sum(weights, axis=-1, keepdims=True)
    acc = jnp.einsum(
        "ipq,iqd->ipd", weights, value.astype(jnp.float32), precision=lax.Precision.HIGHEST
    )
    return (acc / total).astype(jnp.bfloat16).reshape(-1, width)


def after(x, *earlier):
    return lax.optimization_barrier((x, *earlier))[0]


def make_body(mesh):
    n_red, n_wide = mesh.shape["red"], mesh.shape["wide"]
    half_wide = n_wide // 2
    ids = [(wide, core) for wide in range(n_wide) for core in range(2)]

    def swap(x):
        return lax.ppermute(x, "tok", [(0, 1), (1, 0)])

    def sum_red(x):
        total = x.astype(jnp.float32)
        for shift in range(1, n_red):
            pairs = [(i, (i + shift) % n_red) for i in range(n_red)]
            total = total + lax.ppermute(x, "red", pairs).astype(jnp.float32)
        return total

    def sum_holders(x):
        total = x
        n = n_red * 2
        for shift in range(1, n):
            pairs = [(i, (i + shift) % n) for i in range(n)]
            total = total + lax.ppermute(x, ("red", "tok"), pairs)
        return total

    def spread(x):
        got = []
        for k in range(n_wide):
            pairs = []
            for wide, core in ids:
                block = 2 * (wide % half_wide) + core
                target = ((block - k) % n_wide) * 2 + wide // half_wide
                pairs.append((wide * 2 + core, target))
            got.append(lax.ppermute(x, ("wide", "tok"), pairs))
        return jnp.stack(got)

    def collect(pick):
        chip = lax.axis_index("wide")
        total = None
        for k in range(n_wide):
            pairs = []
            for wide, core in ids:
                block = (wide + k) % n_wide
                pairs.append((wide * 2 + core, (core * half_wide + block // 2) * 2 + block % 2))
            got = lax.ppermute(pick((chip + k) % n_wide), ("wide", "tok"), pairs)
            got = got.astype(jnp.float32)
            total = got if total is None else total + got
        return total

    def body(tokens, ln_gain, q_gain, k_gain, w_qkv, w_up, w_attn, w_down):
        core = lax.axis_index("tok")
        chip = lax.axis_index("wide")
        width = tokens.shape[1]
        unit = tokens.shape[0] // sum(SHARES)
        qkv_rows = w_qkv.reshape(w_qkv.shape[0], w_qkv.shape[1] * w_qkv.shape[2])
        attn_rows = w_attn.reshape(w_attn.shape[0] * w_attn.shape[1], w_attn.shape[2])
        piece = w_up.shape[1] // PIECES
        cuts = []
        start = 0
        for share in SHARES:
            cuts.append(slice(start, start + share * unit))
            start += share * unit

        def place(block, image):
            return (2 * block + image - chip) % n_wide

        def take(stack, block, image):
            return lax.dynamic_index_in_dim(stack, place(block, image), 0, keepdims=False)

        raws = [spread(tokens[cut]) for cut in cuts]
        gains = spread(ln_gain)
        gain = jnp.concatenate([take(gains, block, 0) for block in range(half_wide)])

        def normed(raw):
            floats = raw.astype(jnp.float32)
            sums = jnp.stack([jnp.sum(floats, axis=2), jnp.sum(floats * floats, axis=2)], axis=1)
            sums = jnp.stack(
                [
                    sum(take(sums, block, image) for block in range(half_wide))
                    for image in range(2)
                ]
            )
            sums = sum_holders(sums) / D
            groups = []
            for image in (core, 1 - core):
                stat = lax.dynamic_index_in_dim(sums, image, 0, keepdims=False)
                values = jnp.concatenate(
                    [take(raw, block, image) for block in range(half_wide)], axis=1
                ).astype(jnp.float32)
                groups.append(normalize(values, stat[0][:, None], stat[1][:, None], gain))
            return jnp.concatenate(groups, axis=0).astype(jnp.bfloat16)

        def project(x, weight):
            half = x.shape[0] // 2
            part = jnp.dot(x, weight, preferred_element_type=jnp.float32)
            other = swap(part[half:].astype(jnp.bfloat16)).astype(jnp.float32)
            return (part[:half] + other).astype(jnp.bfloat16)

        n = len(cuts)
        inputs = []
        for c in range(n):
            inputs.append(normed(raws[c]))
        sums = [[None] * PIECES for _ in range(n)]
        order = [(c, p) for c in range(n) for p in range(PIECES)]
        done = []
        for at, (c, p) in enumerate(order):
            x = inputs[c] if len(done) < 2 else after(inputs[c], done[-2])
            sums[c][p] = project(x, w_up[:, p * piece : (p + 1) * piece])
            done.append(sums[c][p])
            if at == PIECES:
                pieces = [x[: x.shape[0] // 2] for x in inputs]
                pieces += [x[x.shape[0] // 2 :] for x in inputs]
                qkv = project(after(jnp.concatenate(pieces, axis=0), done[-1]), qkv_rows)
        ups = [[sum_red(s) for s in group] for group in sums]
        attended = attend(sum_red(qkv), q_gain, k_gain)
        attended_other = swap(attended)

        outs = []
        for c, cut in enumerate(cuts):
            rows = cut.stop - cut.start
            both = jnp.concatenate([attended[cut], attended_other[cut]], axis=0)
            terms = jnp.dot(both, attn_rows, preferred_element_type=jnp.float32)
            for p in range(PIECES):
                hidden = jax.nn.gelu(ups[c][p], approximate=False).astype(jnp.bfloat16)
                both = jnp.concatenate([hidden, swap(hidden)], axis=0)
                terms = terms + jnp.dot(
                    both,
                    w_down[p * piece : (p + 1) * piece],
                    preferred_element_type=jnp.float32,
                )
            terms = terms.astype(jnp.bfloat16)

            def pick(block):
                other = (block % 2) ^ core
                return lax.dynamic_slice(
                    terms, (other * rows, (block // 2) * width), (rows, width)
                )

            outs.append(tokens[cut].astype(jnp.float32) + collect(pick))
        return jnp.concatenate(outs, axis=0)

    return body


def solution(mesh):
    return jax.shard_map(
        make_body(mesh),
        mesh=mesh,
        in_specs=(
            P(("grp", "tok"), ("red", "wide")),
            P(("red", "wide")),
            P("wide", None),
            P("wide", None),
            P(("red", "tok"), "wide", None),
            P(("red", "tok"), "wide"),
            P("wide", None, ("red", "tok")),
            P("wide", ("red", "tok")),
        ),
        out_specs=P(("grp", "tok"), ("red", "wide")),
        check_vma=False,
    )
```

time: 255 us -> 226 us (0.89)
  the two profiles are of different devices: /device:TPU:0 before, /device:TPU:12 now
where the time goes in v2:
time: 226 us; the launch traced here: 224 us
  starting transfers between devices  101 us (45%)
  matrix products  52.9 us (23%)
  waiting for transfers between devices  47 us (21%)
  other arithmetic  18.2 us (8%)
  local copies, waits for them, and re-layouts  2.78 us (1%)
    ppermute x16, starting transfers between devices, spread(): got.append(lax.ppermute(x, ('wide', 'tok'), pairs))  39.7 us
    ppermute x12, starting transfers between devices, collect(): got = lax.ppermute(pick((chip + k) % n_wide), ('wide', 'tok'), pairs)  31.1 us
    dot_general x7, matrix products, project(): part = jnp.dot(x, weight, preferred_element_type=jnp.float32)  28.8 us
    dot_general x6, matrix products, body(): jnp.dot(both, w_down[p * piece:(p + 1) * piece], preferred_element_type=j...  22.5 us
    ppermute x7, waiting for transfers between devices, sum_red(): total = total + lax.ppermute(x, 'red', pairs).astype(jnp.float32)  22.2 us
    ppermute x7, starting transfers between devices, sum_red(): total = total + lax.ppermute(x, 'red', pairs).astype(jnp.float32)  18.5 us
    convert_element_type x6, other arithmetic, body(): hidden = jax.nn.gelu(ups[c][p], approximate=False).astype(jnp.bfloat16)  14.1 us
    ppermute x12, waiting for transfers between devices, collect(): got = lax.ppermute(pick((chip + k) % n_wide), ('wide', 'tok'), pairs)  12.2 us
  transfers between devices with their start and end apart: 58, of which 15 were waited for; matrix products, arithmetic and copies ran while one was open for 27% of the time, Pallas kernels for 0%

profile of v2, /device:TPU:12, one launch (start us, length us, event | category | flops | bytes accessed | tf_op | source)
XLA Modules:
  0.0 223.6 jit_solution(12504899103108471454)
XLA Ops:
  0.0 4.6 %collective-permute-start.10 = (bf16[768]{0:T(1024)(128)(2,1)}, bf16[768]{0:T(1024)(128)(2,1)S(1)}, u32[]{:S(2)}, u32[]{:S(2)}) collective-permute-start(bf16[768]{0:T(1024)(128)(2,1)} %param.9), channel_id=1, source_target_pairs={{0,4},{1,8},{4,12},{5,0},{8,5},{9,9},{12,13},{13,1},{2,6},{3,10},{... | collective-permute-start | bytes 4616 | tf_op jit(solution)/shard_map/ppermute | solution.py:74
  10.3 5.0 %collective-permute-start.3 = (bf16[64,768]{1,0:T(8,128)(2,1)S(1)}, bf16[64,768]{1,0:T(8,128)(2,1)S(1)}, u32[]{:S(2)}, u32[]{:S(2)}) collective-permute-start(bf16[64,768]{1,0:T(8,128)(2,1)S(1)} %get-tuple-element.69), channel_id=1, source_target_pairs={{0,4},{1,8},{4,12},{5,0},{8,5},{9,9},{12,13},{13,1},{2,6},{3,10},{... | collective-permute-start | bytes 294920 | tf_op jit(solution)/shard_map/ppermute | solution.py:74
  17.4 5.6 %collective-permute-start = (bf16[64,768]{1,0:T(8,128)(2,1)S(1)}, bf16[64,768]{1,0:T(8,128)(2,1)S(1)}, u32[]{:S(2)}, u32[]{:S(2)}) collective-permute-start(bf16[64,768]{1,0:T(8,128)(2,1)S(1)} %get-tuple-element.69), channel_id=1, source_target_pairs={{0,0},{1,4},{4,8},{5,12},{8,1},{9,5},{12,9},{13,13},{2,2},{3,6},{6... | collective-permute-start | bytes 294920 | tf_op jit(solution)/shard_map/ppermute | solution.py:74
  27.8 4.6 %collective-permute-start.18 = (bf16[64,768]{1,0:T(8,128)(2,1)S(1)}, bf16[64,768]{1,0:T(8,128)(2,1)S(1)}, u32[]{:S(2)}, u32[]{:S(2)}) collective-permute-start(bf16[64,768]{1,0:T(8,128)(2,1)S(1)} %get-tuple-element.68), channel_id=1, source_target_pairs={{0,0},{1,4},{4,8},{5,12},{8,1},{9,5},{12,9},{13,13},{2,2},{3,6},{6... | collective-permute-start | bytes 294920 | tf_op jit(solution)/shard_map/ppermute | solution.py:74
  32.4 3.8 %collective-permute-start.14 = (bf16[128,768]{1,0:T(8,128)(2,1)S(1)}, bf16[128,768]{1,0:T(8,128)(2,1)S(1)}, u32[]{:S(2)}, u32[]{:S(2)}) collective-permute-start(bf16[128,768]{1,0:T(8,128)(2,1)S(1)} %slice.188), channel_id=1, source_target_pairs={{0,4},{1,8},{4,12},{5,0},{8,5},{9,9},{12,13},{13,1},{2,6},{3,10},{... | collective-permute-start | bytes 589832 | tf_op jit(solution)/shard_map/ppermute | solution.py:74
  45.6 5.2 %collective-permute-start.11 = (bf16[128,768]{1,0:T(8,128)(2,1)S(1)}, bf16[128,768]{1,0:T(8,128)(2,1)S(1)}, u32[]{:S(2)}, u32[]{:S(2)}) collective-permute-start(bf16[128,768]{1,0:T(8,128)(2,1)S(1)} %slice.188), channel_id=1, source_target_pairs={{0,0},{1,4},{4,8},{5,12},{8,1},{9,5},{12,9},{13,13},{2,2},{3,6},{6... | collective-permute-start | bytes 589832 | tf_op jit(solution)/shard_map/ppermute | solution.py:74
  51.1 5.3 %collective-permute-done.11 = bf16[128,768]{1,0:T(8,128)(2,1)S(1)} collective-permute-done((bf16[128,768]{1,0:T(8,128)(2,1)S(1)}, bf16[128,768]{1,0:T(8,128)(2,1)S(1)}, u32[]{:S(2)}, u32[]{:S(2)}) %collective-permute-start.11) | collective-permute-done | bytes 196640 | tf_op jit(solution)/shard_map/ppermute | solution.py:74
  64.0 5.2 %fusion.10 = f32[128,3072]{1,0:T(8,128)S(1)} fusion(bf16[1536,6144]{1,0:T(8,128)(2,1)} %param.13, bf16[64,1536]{1,0:T(8,128)(2,1)S(1)} %get-tuple-element.32, bf16[64,1536]{1,0:T(8,128)(2,1)S(1)} %get-tuple-element.38), kind=kOutput, calls=%fused_computation.10 | convolution fusion | flops 1208745984 | bytes 11403264 | tf_op jit(solution)/shard_map/dot_general | solution.py:135
  69.3 5.2 %fusion.22 = f32[128,3072]{1,0:T(8,128)S(1)} fusion(bf16[1536,6144]{1,0:T(8,128)(2,1)} %param.13, bf16[64,1536]{1,0:T(8,128)(2,1)S(1)} %get-tuple-element.32, bf16[64,1536]{1,0:T(8,128)(2,1)S(1)} %get-tuple-element.38), kind=kOutput, calls=%fused_computation.22 | convolution fusion | flops 1208745984 | bytes 11403264 | tf_op jit(solution)/shard_map/dot_general | solution.py:135
  78.7 5.2 %fusion.20 = f32[256,3072]{1,0:T(8,128)S(1)} fusion(bf16[256,1536]{1,0:T(8,128)(2,1)S(1)} %pad_maximum_fusion.1, bf16[1536,6144]{1,0:T(8,128)(2,1)} %param.13), kind=kOutput, calls=%fused_computation.20 | convolution fusion | flops 2415919104 | bytes 13369344 | tf_op jit(solution)/shard_map/dot_general | solution.py:135
  84.1 5.5 %fusion.8 = f32[256,3072]{1,0:T(8,128)S(1)} fusion(bf16[256,1536]{1,0:T(8,128)(2,1)S(1)} %pad_maximum_fusion.1, bf16[1536,6144]{1,0:T(8,128)(2,1)} %param.13), kind=kOutput, calls=%fused_computation.8 | convolution fusion | flops 2415919104 | bytes 13369344 | tf_op jit(solution)/shard_map/dot_general | solution.py:135
  92.0 4.1 %collective-permute-done.30 = bf16[64,3072]{1,0:T(8,128)(2,1)S(1)} collective-permute-done((bf16[64,3072]{1,0:T(8,128)(2,1)S(1)}, bf16[64,3072]{1,0:T(8,128)(2,1)S(1)}, u32[]{:S(2)}, u32[]{:S(2)}) %collective-permute-start.30) | collective-permute-done | bytes 393248 | tf_op jit(solution)/shard_map/ppermute | solution.py:55
  101.4 5.5 %fusion.6 = f32[128,3072]{1,0:T(8,128)S(1)} fusion(bf16[128,1536]{1,0:T(8,128)(2,1)S(1)} %pad_maximum_fusion.6, bf16[1536,6144]{1,0:T(8,128)(2,1)} %param.13), kind=kOutput, calls=%fused_computation.6 | convolution fusion | flops 1207959552 | bytes 11403264 | tf_op jit(solution)/shard_map/dot_general | solution.py:135
  107.8 5.4 %fusion.4 = f32[128,1536]{1,0:T(8,128)S(1)} fusion(bf16[6144,1536]{1,0:T(8,128)(2,1)} %param.15, bf16[64,3072]{1,0:T(8,128)(2,1)S(1)} %collective-permute-done.34, bf16[64,3072]{1,0:T(8,128)(2,1)S(1)} %fusion.69), kind=kOutput, calls=%fused_computation.4 | convolution fusion | flops 1209532416 | bytes 11010048 | tf_op jit(solution)/shard_map/dot_general | solution.py:166
  115.8 5.2 %fusion.16 = f32[128,1536]{1,0:T(8,128)S(1)} fusion(bf16[6144,1536]{1,0:T(8,128)(2,1)} %param.15, bf16[64,3072]{1,0:T(8,128)(2,1)S(1)} %collective-permute-done.31, bf16[64,3072]{1,0:T(8,128)(2,1)S(1)} %fusion.66), kind=kOutput, calls=%fused_computation.16 | convolution fusion | flops 1209532416 | bytes 11010048 | tf_op jit(solution)/shard_map/dot_general | solution.py:166
  121.1 18.1 %collective-permute-done.28 = bf16[256,384]{0,1:T(8,128)(2,1)S(1)} collective-permute-done((bf16[256,384]{0,1:T(8,128)(2,1)S(1)}, bf16[256,384]{0,1:T(8,128)(2,1)S(1)}, u32[]{:S(2)}, u32[]{:S(2)}) %collective-permute-start.28) | collective-permute-done | bytes 196640 | tf_op jit(solution)/shard_map/ppermute | solution.py:55
  141.3 12.3 %collective-permute-start.49 = (bf16[64,3072]{1,0:T(8,128)(2,1)S(1)}, bf16[64,3072]{1,0:T(8,128)(2,1)S(1)}, u32[]{:S(2)}, u32[]{:S(2)}) collective-permute-start(bf16[64,3072]{1,0:T(8,128)(2,1)S(1)} %fusion.77), channel_id=1, source_target_pairs={{0,2},{2,0},{1,3},{3,1},{4,6},{6,4},{5,7},{7,5},{8,10},{10,8},{9,1... | collective-permute-start | bytes 1179656 | tf_op jit(solution)/shard_map/ppermute | solution.py:55
  156.7 3.5 %fusion.36 = bf16[128,3072]{1,0:T(8,128)(2,1)S(1)} fusion(bf16[128,3072]{1,0:T(8,128)(2,1)S(1)} %collective-permute-done.42, bf16[128,3072]{1,0:T(8,128)(2,1)S(1)} %fusion.37), kind=kLoop, calls=%fused_computation.43 | loop fusion | flops 26738688 | bytes 2359296 | tf_op jit(solution)/shard_map/convert_element_type | solution.py:164
  161.0 3.5 %fusion.33 = bf16[128,3072]{1,0:T(8,128)(2,1)S(1)} fusion(bf16[128,3072]{1,0:T(8,128)(2,1)S(1)} %collective-permute-done.39, bf16[128,3072]{1,0:T(8,128)(2,1)S(1)} %fusion.38), kind=kLoop, calls=%fused_computation.40 | loop fusion | flops 26738688 | bytes 2359296 | tf_op jit(solution)/shard_map/convert_element_type | solution.py:164
  164.6 6.7 %collective-permute-start.35 = (bf16[64,768]{1,0:T(8,128)(2,1)S(1)}, bf16[64,768]{1,0:T(8,128)(2,1)S(1)}, u32[]{:S(2)}, u32[]{:S(2)}) collective-permute-start(bf16[64,768]{1,0:T(8,128)(2,1)S(1)} %get-tuple-element.52), channel_id=1, source_target_pairs={{0,0},{1,8},{4,1},{5,9},{8,4},{9,12},{12,5},{13,13},{2,2},{3,10},{... | collective-permute-start | bytes 294920 | tf_op jit(solution)/shard_map/ppermute | solution.py:85
  175.5 5.4 %fusion = f32[128,1536]{1,0:T(8,128)S(1)} fusion(bf16[6144,1536]{1,0:T(8,128)(2,1)} %param.15, bf16[64,3072]{1,0:T(8,128)(2,1)S(1)} %collective-permute-done.53, bf16[64,3072]{1,0:T(8,128)(2,1)S(1)} %fusion.75), kind=kOutput, calls=%fused_computation | convolution fusion | flops 1209532416 | bytes 11010048 | tf_op jit(solution)/shard_map/dot_general | solution.py:166
  193.2 5.7 %collective-permute-start.54 = (bf16[64,768]{1,0:T(8,128)(2,1)S(1)}, bf16[64,768]{1,0:T(8,128)(2,1)S(1)}, u32[]{:S(2)}, u32[]{:S(2)}) collective-permute-start(bf16[64,768]{1,0:T(8,128)(2,1)S(1)} %get-tuple-element.56), channel_id=1, source_target_pairs={{0,0},{1,8},{4,1},{5,9},{8,4},{9,12},{12,5},{13,13},{2,2},{3,10},{... | collective-permute-start | bytes 294920 | tf_op jit(solution)/shard_map/ppermute | solution.py:85
  203.2 6.9 %collective-permute-start.44 = (bf16[128,768]{1,0:T(8,128)(2,1)S(1)}, bf16[128,768]{1,0:T(8,128)(2,1)S(1)}, u32[]{:S(2)}, u32[]{:S(2)}) collective-permute-start(bf16[128,768]{1,0:T(8,128)(2,1)S(1)} %get-tuple-element.42), channel_id=1, source_target_pairs={{0,0},{1,8},{4,1},{5,9},{8,4},{9,12},{12,5},{13,13},{2,2},{3,10},{... | collective-permute-start | bytes 589832 | tf_op jit(solution)/shard_map/ppermute | solution.py:85
  212.0 10.3 %collective-permute-done.44 = bf16[128,768]{1,0:T(8,128)(2,1)S(1)} collective-permute-done((bf16[128,768]{1,0:T(8,128)(2,1)S(1)}, bf16[128,768]{1,0:T(8,128)(2,1)S(1)}, u32[]{:S(2)}, u32[]{:S(2)}) %collective-permute-start.44) | collective-permute-done | bytes 196640 | tf_op jit(solution)/shard_map/ppermute | solution.py:85
  (225 shorter events, 73.9 us)
Async XLA Ops:
  0.0 16.6 %collective-permute-start.10 = (bf16[768]{0:T(1024)(128)(2,1)}, bf16[768]{0:T(1024)(128)(2,1)S(1)}, u32[]{:S(2)}, u32[]{:S(2)}) collective-permute-start(bf16[768]{0:T(1024)(128)(2,1)} %param.9), channel_id=1, source_target_pairs={{0,4},{1,8},{4,12},{5,0},{8,5},{9,9},{12,13},{13,1},{2,6},{3,10},{... | collective-permute-start | bytes 4616 | tf_op jit(solution)/shard_map/ppermute | solution.py:74
  6.0 17.0 %collective-permute-start.7 = (bf16[768]{0:T(1024)(128)(2,1)}, bf16[768]{0:T(1024)(128)(2,1)S(1)}, u32[]{:S(2)}, u32[]{:S(2)}) collective-permute-start(bf16[768]{0:T(1024)(128)(2,1)} %param.9), channel_id=1, source_target_pairs={{0,0},{1,4},{4,8},{5,12},{8,1},{9,5},{12,9},{13,13},{2,2},{3,6},{6... | collective-permute-start | bytes 4616 | tf_op jit(solution)/shard_map/ppermute | solution.py:74
  10.3 16.1 %collective-permute-start.3 = (bf16[64,768]{1,0:T(8,128)(2,1)S(1)}, bf16[64,768]{1,0:T(8,128)(2,1)S(1)}, u32[]{:S(2)}, u32[]{:S(2)}) collective-permute-start(bf16[64,768]{1,0:T(8,128)(2,1)S(1)} %get-tuple-element.69), channel_id=1, source_target_pairs={{0,4},{1,8},{4,12},{5,0},{8,5},{9,9},{12,13},{13,1},{2,6},{3,10},{... | collective-permute-start | bytes 294920 | tf_op jit(solution)/shard_map/ppermute | solution.py:74
  17.4 15.1 %collective-permute-start = (bf16[64,768]{1,0:T(8,128)(2,1)S(1)}, bf16[64,768]{1,0:T(8,128)(2,1)S(1)}, u32[]{:S(2)}, u32[]{:S(2)}) collective-permute-start(bf16[64,768]{1,0:T(8,128)(2,1)S(1)} %get-tuple-element.69), channel_id=1, source_target_pairs={{0,0},{1,4},{4,8},{5,12},{8,1},{9,5},{12,9},{13,13},{2,2},{3,6},{6... | collective-permute-start | bytes 294920 | tf_op jit(solution)/shard_map/ppermute | solution.py:74
  32.4 18.6 %collective-permute-start.14 = (bf16[128,768]{1,0:T(8,128)(2,1)S(1)}, bf16[128,768]{1,0:T(8,128)(2,1)S(1)}, u32[]{:S(2)}, u32[]{:S(2)}) collective-permute-start(bf16[128,768]{1,0:T(8,128)(2,1)S(1)} %slice.188), channel_id=1, source_target_pairs={{0,4},{1,8},{4,12},{5,0},{8,5},{9,9},{12,13},{13,1},{2,6},{3,10},{... | collective-permute-start | bytes 589832 | tf_op jit(solution)/shard_map/ppermute | solution.py:74
  36.4 14.6 %collective-permute-start.13 = (bf16[128,768]{1,0:T(8,128)(2,1)S(1)}, bf16[128,768]{1,0:T(8,128)(2,1)S(1)}, u32[]{:S(2)}, u32[]{:S(2)}) collective-permute-start(bf16[128,768]{1,0:T(8,128)(2,1)S(1)} %slice.188), channel_id=1, source_target_pairs={{0,8},{1,12},{4,0},{5,4},{8,9},{9,13},{12,1},{13,5},{2,10},{3,14},... | collective-permute-start | bytes 589832 | tf_op jit(solution)/shard_map/ppermute | solution.py:74
  77.5 18.6 %collective-permute-start.30 = (bf16[64,3072]{1,0:T(8,128)(2,1)S(1)}, bf16[64,3072]{1,0:T(8,128)(2,1)S(1)}, u32[]{:S(2)}, u32[]{:S(2)}) collective-permute-start(bf16[64,3072]{1,0:T(8,128)(2,1)S(1)} %fusion.79), channel_id=1, source_target_pairs={{0,2},{2,0},{1,3},{3,1},{4,6},{6,4},{5,7},{7,5},{8,10},{10,8},{9,1... | collective-permute-start | bytes 1179656 | tf_op jit(solution)/shard_map/ppermute | solution.py:55
  84.0 15.1 %collective-permute-start.26 = (bf16[128,3072]{1,0:T(8,128)(2,1)S(1)}, bf16[128,3072]{1,0:T(8,128)(2,1)S(1)}, u32[]{:S(2)}, u32[]{:S(2)}) collective-permute-start(bf16[128,3072]{1,0:T(8,128)(2,1)S(1)} %slice.357), channel_id=1, source_target_pairs={{0,1},{1,0},{2,3},{3,2},{4,5},{5,4},{6,7},{7,6},{8,9},{9,8},{10,11... | collective-permute-start | bytes 2359304 | tf_op jit(solution)/shard_map/ppermute | solution.py:49
  91.9 15.1 %collective-permute-start.34 = (bf16[64,3072]{1,0:T(8,128)(2,1)S(1)}, bf16[64,3072]{1,0:T(8,128)(2,1)S(1)}, u32[]{:S(2)}, u32[]{:S(2)}) collective-permute-start(bf16[64,3072]{1,0:T(8,128)(2,1)S(1)} %fusion.69), channel_id=1, source_target_pairs={{0,1},{1,0},{2,3},{3,2},{4,5},{5,4},{6,7},{7,6},{8,9},{9,8},{10,11... | collective-permute-start | bytes 1179656 | tf_op jit(solution)/shard_map/ppermute | solution.py:49
  97.8 17.1 %collective-permute-start.31 = (bf16[64,3072]{1,0:T(8,128)(2,1)S(1)}, bf16[64,3072]{1,0:T(8,128)(2,1)S(1)}, u32[]{:S(2)}, u32[]{:S(2)}) collective-permute-start(bf16[64,3072]{1,0:T(8,128)(2,1)S(1)} %fusion.66), channel_id=1, source_target_pairs={{0,1},{1,0},{2,3},{3,2},{4,5},{5,4},{6,7},{7,6},{8,9},{9,8},{10,11... | collective-permute-start | bytes 1179656 | tf_op jit(solution)/shard_map/ppermute | solution.py:49
  98.1 58.5 %collective-permute-start.42 = (bf16[128,3072]{1,0:T(8,128)(2,1)S(1)}, bf16[128,3072]{1,0:T(8,128)(2,1)S(1)}, u32[]{:S(2)}, u32[]{:S(2)}) collective-permute-start(bf16[128,3072]{1,0:T(8,128)(2,1)S(1)} %fusion.37), channel_id=1, source_target_pairs={{0,2},{2,0},{1,3},{3,1},{4,6},{6,4},{5,7},{7,5},{8,10},{10,8},{9,1... | collective-permute-start | bytes 2359304 | tf_op jit(solution)/shard_map/ppermute | solution.py:55
  99.2 61.0 %collective-permute-start.39 = (bf16[128,3072]{1,0:T(8,128)(2,1)S(1)}, bf16[128,3072]{1,0:T(8,128)(2,1)S(1)}, u32[]{:S(2)}, u32[]{:S(2)}) collective-permute-start(bf16[128,3072]{1,0:T(8,128)(2,1)S(1)} %fusion.38), channel_id=1, source_target_pairs={{0,2},{2,0},{1,3},{3,1},{4,6},{6,4},{5,7},{7,5},{8,10},{10,8},{9,1... | collective-permute-start | bytes 2359304 | tf_op jit(solution)/shard_map/ppermute | solution.py:55
  107.0 33.2 %collective-permute-start.51 = (bf16[64,3072]{1,0:T(8,128)(2,1)S(1)}, bf16[64,3072]{1,0:T(8,128)(2,1)S(1)}, u32[]{:S(2)}, u32[]{:S(2)}) collective-permute-start(bf16[64,3072]{1,0:T(8,128)(2,1)S(1)} %slice.358), channel_id=1, source_target_pairs={{0,1},{1,0},{2,3},{3,2},{4,5},{5,4},{6,7},{7,6},{8,9},{9,8},{10,11... | collective-permute-start | bytes 1179656 | tf_op jit(solution)/shard_map/ppermute | solution.py:49
  114.7 26.6 %collective-permute-start.48 = (bf16[64,3072]{1,0:T(8,128)(2,1)S(1)}, bf16[64,3072]{1,0:T(8,128)(2,1)S(1)}, u32[]{:S(2)}, u32[]{:S(2)}) collective-permute-start(bf16[64,3072]{1,0:T(8,128)(2,1)S(1)} %slice.359), channel_id=1, source_target_pairs={{0,1},{1,0},{2,3},{3,2},{4,5},{5,4},{6,7},{7,6},{8,9},{9,8},{10,11... | collective-permute-start | bytes 1179656 | tf_op jit(solution)/shard_map/ppermute | solution.py:49
  114.9 24.3 %collective-permute-start.28 = (bf16[256,384]{0,1:T(8,128)(2,1)S(1)}, bf16[256,384]{0,1:T(8,128)(2,1)S(1)}, u32[]{:S(2)}, u32[]{:S(2)}) collective-permute-start(bf16[256,384]{0,1:T(8,128)(2,1)S(1)} %fusion.120), channel_id=1, source_target_pairs={{0,2},{2,0},{1,3},{3,1},{4,6},{6,4},{5,7},{7,5},{8,10},{10,8},{9,1... | collective-permute-start | bytes 589832 | tf_op jit(solution)/shard_map/ppermute | solution.py:55
  140.3 24.3 %collective-permute-start.52 = (bf16[64,3072]{1,0:T(8,128)(2,1)S(1)}, bf16[64,3072]{1,0:T(8,128)(2,1)S(1)}, u32[]{:S(2)}, u32[]{:S(2)}) collective-permute-start(bf16[64,3072]{1,0:T(8,128)(2,1)S(1)} %fusion.76), channel_id=1, source_target_pairs={{0,2},{2,0},{1,3},{3,1},{4,6},{6,4},{5,7},{7,5},{8,10},{10,8},{9,1... | collective-permute-start | bytes 1179656 | tf_op jit(solution)/shard_map/ppermute | solution.py:55
  141.3 31.7 %collective-permute-start.49 = (bf16[64,3072]{1,0:T(8,128)(2,1)S(1)}, bf16[64,3072]{1,0:T(8,128)(2,1)S(1)}, u32[]{:S(2)}, u32[]{:S(2)}) collective-permute-start(bf16[64,3072]{1,0:T(8,128)(2,1)S(1)} %fusion.77), channel_id=1, source_target_pairs={{0,2},{2,0},{1,3},{3,1},{4,6},{6,4},{5,7},{7,5},{8,10},{10,8},{9,1... | collective-permute-start | bytes 1179656 | tf_op jit(solution)/shard_map/ppermute | solution.py:55
  154.0 37.2 %collective-permute-start.38 = (bf16[64,768]{1,0:T(8,128)(2,1)S(1)}, bf16[64,768]{1,0:T(8,128)(2,1)S(1)}, u32[]{:S(2)}, u32[]{:S(2)}) collective-permute-start(bf16[64,768]{1,0:T(8,128)(2,1)S(1)} %get-tuple-element.53), channel_id=1, source_target_pairs={{0,5},{1,13},{4,0},{5,8},{8,1},{9,9},{12,4},{13,12},{2,7},{3,15},{... | collective-permute-start | bytes 294920 | tf_op jit(solution)/shard_map/ppermute | solution.py:85
  156.6 35.9 %collective-permute-start.37 = (bf16[64,768]{1,0:T(8,128)(2,1)S(1)}, bf16[64,768]{1,0:T(8,128)(2,1)S(1)}, u32[]{:S(2)}, u32[]{:S(2)}) collective-permute-start(bf16[64,768]{1,0:T(8,128)(2,1)S(1)} %get-tuple-element.54), channel_id=1, source_target_pairs={{0,4},{1,12},{4,5},{5,13},{8,0},{9,8},{12,1},{13,9},{2,6},{3,14},{... | collective-permute-start | bytes 294920 | tf_op jit(solution)/shard_map/ppermute | solution.py:85
  160.2 32.9 %collective-permute-start.36 = (bf16[64,768]{1,0:T(8,128)(2,1)S(1)}, bf16[64,768]{1,0:T(8,128)(2,1)S(1)}, u32[]{:S(2)}, u32[]{:S(2)}) collective-permute-start(bf16[64,768]{1,0:T(8,128)(2,1)S(1)} %get-tuple-element.55), channel_id=1, source_target_pairs={{0,1},{1,9},{4,4},{5,12},{8,5},{9,13},{12,0},{13,8},{2,3},{3,11},{... | collective-permute-start | bytes 294920 | tf_op jit(solution)/shard_map/ppermute | solution.py:85
  164.6 34.3 %collective-permute-start.35 = (bf16[64,768]{1,0:T(8,128)(2,1)S(1)}, bf16[64,768]{1,0:T(8,128)(2,1)S(1)}, u32[]{:S(2)}, u32[]{:S(2)}) collective-permute-start(bf16[64,768]{1,0:T(8,128)(2,1)S(1)} %get-tuple-element.52), channel_id=1, source_target_pairs={{0,0},{1,8},{4,1},{5,9},{8,4},{9,12},{12,5},{13,13},{2,2},{3,10},{... | collective-permute-start | bytes 294920 | tf_op jit(solution)/shard_map/ppermute | solution.py:85
  185.9 14.9 %collective-permute-start.57 = (bf16[64,768]{1,0:T(8,128)(2,1)S(1)}, bf16[64,768]{1,0:T(8,128)(2,1)S(1)}, u32[]{:S(2)}, u32[]{:S(2)}) collective-permute-start(bf16[64,768]{1,0:T(8,128)(2,1)S(1)} %get-tuple-element.57), channel_id=1, source_target_pairs={{0,5},{1,13},{4,0},{5,8},{8,1},{9,9},{12,4},{13,12},{2,7},{3,15},{... | collective-permute-start | bytes 294920 | tf_op jit(solution)/shard_map/ppermute | solution.py:85
  193.2 16.9 %collective-permute-start.54 = (bf16[64,768]{1,0:T(8,128)(2,1)S(1)}, bf16[64,768]{1,0:T(8,128)(2,1)S(1)}, u32[]{:S(2)}, u32[]{:S(2)}) collective-permute-start(bf16[64,768]{1,0:T(8,128)(2,1)S(1)} %get-tuple-element.56), channel_id=1, source_target_pairs={{0,0},{1,8},{4,1},{5,9},{8,4},{9,12},{12,5},{13,13},{2,2},{3,10},{... | collective-permute-start | bytes 294920 | tf_op jit(solution)/shard_map/ppermute | solution.py:85
  203.2 19.2 %collective-permute-start.44 = (bf16[128,768]{1,0:T(8,128)(2,1)S(1)}, bf16[128,768]{1,0:T(8,128)(2,1)S(1)}, u32[]{:S(2)}, u32[]{:S(2)}) collective-permute-start(bf16[128,768]{1,0:T(8,128)(2,1)S(1)} %get-tuple-element.42), channel_id=1, source_target_pairs={{0,0},{1,8},{4,1},{5,9},{8,4},{9,12},{12,5},{13,13},{2,2},{3,10},{... | collective-permute-start | bytes 589832 | tf_op jit(solution)/shard_map/ppermute | solution.py:85
  (52 other events, 722.2 us)

commit v3 on v1

v3 whole, which is shorter than its diff:
```python
import functools
import math

import jax
import jax.numpy as jnp
from jax import lax
from jax.experimental import pallas as pl
from jax.experimental.pallas import tpu as pltpu
from jax.sharding import PartitionSpec as P

D = 6144
PATCHES = 256
EPS = 1e-06
SHARES = (7, 5, 4)
PIECES = (2, 1)
GAIN_ROWS = 8


def normalize(values, mean, meansq, gain):
    return (values - mean) * lax.rsqrt(meansq - mean * mean + EPS) * gain.astype(jnp.float32)


def head_norm(values, gain):
    mean = jnp.mean(values, axis=-1, keepdims=True)
    meansq = jnp.mean(values * values, axis=-1, keepdims=True)
    return normalize(values, mean, meansq, gain)


def attend(qkv, q_gain, k_gain):
    width = q_gain.shape[1]
    query = head_norm(qkv[:, :width], q_gain[0]).astype(jnp.bfloat16)
    key = head_norm(qkv[:, width : 2 * width], k_gain[0]).astype(jnp.bfloat16)
    value = qkv[:, 2 * width :].astype(jnp.bfloat16)
    query, key, value = (a.reshape(-1, PATCHES, width) for a in (query, key, value))
    scores = jnp.einsum("ipd,iqd->ipq", query, key, preferred_element_type=jnp.float32)
    scores = scores * width ** (-0.5)
    weights = jnp.exp(scores - jnp.max(scores, axis=-1, keepdims=True))
    total = jnp.sum(weights, axis=-1, keepdims=True)
    acc = jnp.einsum(
        "ipq,iqd->ipd", weights, value.astype(jnp.float32), precision=lax.Precision.HIGHEST
    )
    return (acc / total).astype(jnp.bfloat16).reshape(-1, width)


def nothing(x):
    corner = x[(0,) * x.ndim].astype(jnp.int32)
    return lax.shift_right_logical(corner & 1, 1).astype(jnp.float32)


def slices(size, shares):
    ends = [sum(shares[: i + 1]) * size // sum(shares) for i in range(len(shares))]
    return [slice(a, b) for a, b in zip([0] + ends[:-1], ends)]


def block_of(size):
    return next(b for b in (512, 384, 256, 128) if size % b == 0)


PARAMS = pltpu.CompilerParams(vmem_limit_bytes=20 * 2**20)
SOON = pl.CostEstimate(flops=0, bytes_accessed=0, transcendentals=0)
WHOLE = pl.BlockSpec(memory_space=pl.ANY)


def project_kernel(n_earlier, own_ref, other_ref, w_ref, *refs):
    near_ref, far_ref, x_ref = refs[n_earlier:]
    rows = own_ref.shape[0]

    @pl.when(pl.program_id(0) == 0)
    def _():
        x_ref[:rows] = own_ref[...]
        x_ref[rows:] = other_ref[...]

    part = jnp.dot(x_ref[...], w_ref[...], preferred_element_type=jnp.float32)
    near_ref[...] = part[:rows]
    far_ref[...] = part[rows:].astype(jnp.bfloat16)


def project_tokens(own, other, weight, piece, earlier):
    rows, depth = own.shape
    columns = piece.stop - piece.start
    block = block_of(math.gcd(columns, piece.start))
    steps, skipped = columns // block, piece.start // block
    whole = pl.BlockSpec((rows, depth), lambda j: (0, 0))
    out = pl.BlockSpec((rows, block), lambda j: (0, j))
    return pl.pallas_call(
        functools.partial(project_kernel, len(earlier)),
        grid=(steps,),
        in_specs=[
            whole,
            whole,
            pl.BlockSpec((depth, block), lambda j: (0, skipped + j)),
        ]
        + [WHOLE] * len(earlier),
        out_specs=[out, out],
        out_shape=[
            jax.ShapeDtypeStruct((rows, columns), jnp.float32),
            jax.ShapeDtypeStruct((rows, columns), jnp.bfloat16),
        ],
        scratch_shapes=[pltpu.VMEM((2 * rows, depth), jnp.bfloat16)],
        compiler_params=PARAMS,
        cost_estimate=SOON,
    )(own, other, weight, *earlier)


def output_kernel(n_added, n_earlier, own_ref, other_ref, w_ref, *refs):
    added = refs[:n_added]
    out_ref, total_ref = refs[n_added + n_earlier :]
    k = pl.program_id(0)
    hidden = jnp.concatenate([own_ref[...], other_ref[...]], axis=0)
    part = jnp.dot(hidden, w_ref[...], preferred_element_type=jnp.float32)

    @pl.when(k == 0)
    def _():
        total_ref[...] = sum([a[...] for a in added], part)

    @pl.when(k > 0)
    def _():
        total_ref[...] += part

    @pl.when(k == pl.num_programs(0) - 1)
    def _():
        out_ref[...] = total_ref[...].astype(out_ref.dtype)


def project_hidden(own, other, weight, piece, added, dtype, earlier):
    rows, units = own.shape
    columns = weight.shape[1]
    block = block_of(math.gcd(units, piece.start))
    steps, skipped = units // block, piece.start // block
    whole = pl.BlockSpec((2 * rows, columns), lambda k: (0, 0))
    part = pl.BlockSpec((rows, block), lambda k: (0, k))
    return pl.pallas_call(
        functools.partial(output_kernel, len(added), len(earlier)),
        grid=(steps,),
        in_specs=[
            part,
            part,
            pl.BlockSpec((block, columns), lambda k: (skipped + k, 0)),
        ]
        + [whole] * len(added)
        + [WHOLE] * len(earlier),
        out_specs=whole,
        out_shape=jax.ShapeDtypeStruct((2 * rows, columns), dtype),
        scratch_shapes=[pltpu.VMEM((2 * rows, columns), jnp.float32)],
        compiler_params=PARAMS,
        cost_estimate=SOON,
    )(own, other, weight, *added, *earlier)


def make_body(mesh):
    n_red, n_wide = mesh.shape["red"], mesh.shape["wide"]

    def swap(x):
        return lax.ppermute(x, "tok", [(0, 1), (1, 0)])

    def sum_red(x):
        total = x.astype(jnp.float32)
        for shift in range(1, n_red):
            pairs = [(i, (i + shift) % n_red) for i in range(n_red)]
            total = total + lax.ppermute(x, "red", pairs).astype(jnp.float32)
        return total

    def collect(x, width):
        chip = lax.axis_index("wide")
        total = lax.dynamic_slice_in_dim(x, chip * width, width, axis=1).astype(jnp.float32)
        for k in range(n_wide - 1, 0, -1):
            sent = lax.dynamic_slice_in_dim(x, (chip ^ k) * width, width, axis=1)
            got = lax.ppermute(sent, "wide", [(i, i ^ k) for i in range(n_wide)])
            total = total + got.astype(jnp.float32)
        return total

    def body(tokens, ln_gain, q_gain, k_gain, w_qkv, w_up, w_attn, w_down):
        core = lax.axis_index("tok")
        width = tokens.shape[1]
        qkv_rows = w_qkv.reshape(w_qkv.shape[0], w_qkv.shape[1] * w_qkv.shape[2])
        attn_rows = w_attn.reshape(w_attn.shape[0] * w_attn.shape[1], w_attn.shape[2])
        depth = w_up.shape[0]
        cuts = slices(tokens.shape[0], SHARES)
        pieces = slices(w_up.shape[1], PIECES)
        first = cuts[0].stop

        gain_rows = jnp.broadcast_to(ln_gain[None], (GAIN_ROWS, width))
        lead = jnp.concatenate([gain_rows, tokens[:first]], axis=0)
        lead = lax.all_gather(lead, "wide", axis=1, tiled=True)
        gain = lead[:1]

        def normed(floats):
            sums = jnp.stack([jnp.sum(floats, axis=1), jnp.sum(floats * floats, axis=1)])
            sums = sum_red(sums)[:, :, None] / D
            values = normalize(floats, sums[0], sums[1], gain).astype(jnp.bfloat16)
            mine = lax.dynamic_slice_in_dim(values, core * depth, depth, axis=1)
            theirs = lax.dynamic_slice_in_dim(values, (1 - core) * depth, depth, axis=1)
            return mine, swap(theirs)

        n = len(cuts)
        pairs = [normed(lead[GAIN_ROWS:].astype(jnp.float32))]
        sums, ups = [], [[] for _ in range(n)]
        qkv = None
        for c in range(n):
            if c == 1:
                rest = tokens[first:] + nothing(sums[-1]).astype(jnp.bfloat16)
                rest = lax.all_gather(rest, "wide", axis=1, tiled=True)
                rest_pair = normed(rest.astype(jnp.float32) + nothing(ups[0][0]))
                for cut in cuts[1:]:
                    part = slice(cut.start - first, cut.stop - first)
                    pairs.append([a[part] for a in rest_pair])
                own, other = (
                    jnp.concatenate([a, b], axis=0) for a, b in zip(pairs[0], rest_pair)
                )
                near, far = project_tokens(own, other, qkv_rows, slice(0, qkv_rows.shape[1]), ())
                qkv = (near + swap(far).astype(jnp.float32)).astype(jnp.bfloat16)
            for piece in pieces:
                near, far = project_tokens(*pairs[c], w_up, piece, sums[-2:-1])
                sums.append((near + swap(far).astype(jnp.float32)).astype(jnp.bfloat16))
                ups[c].append(sum_red(sums[-1]))
        ups[0][1] = ups[0][1] + nothing(sums[-1])
        attended = attend(sum_red(qkv), q_gain, k_gain)
        attended_other = swap(attended)

        outs = []
        for c, cut in enumerate(cuts):
            rows = cut.stop - cut.start
            both = jnp.concatenate([attended[cut], attended_other[cut]], axis=0)
            added = [jnp.dot(both, attn_rows, preferred_element_type=jnp.float32)]
            terms = None
            if c == n - 1 and n > 2:
                ups[c][0] = ups[c][0] + nothing(outs[0])
            for p, piece in enumerate(pieces):
                hidden = jax.nn.gelu(ups[c][p], approximate=False).astype(jnp.bfloat16)
                last = p == len(pieces) - 1
                terms = project_hidden(
                    hidden,
                    swap(hidden),
                    w_down,
                    piece,
                    ([] if terms is None else [terms]) + (added if last else []),
                    jnp.bfloat16 if last else jnp.float32,
                    (),
                )
            kept, got = terms[:rows], swap(terms[rows:])
            lower = jnp.where(core == 0, kept, got)
            upper = jnp.where(core == 0, got, kept)
            terms = jnp.concatenate([lower, upper], axis=1)
            if c < n - 1:
                summed = lax.psum_scatter(terms, "wide", scatter_dimension=1, tiled=True)
                summed = summed.astype(jnp.float32)
            else:
                summed = collect(terms, width)
            outs.append(tokens[cut].astype(jnp.float32) + summed)
        return jnp.concatenate(outs, axis=0)

    return body


def solution(mesh):
    return jax.shard_map(
        make_body(mesh),
        mesh=mesh,
        in_specs=(
            P(("grp", "tok"), ("red", "wide")),
            P(("red", "wide")),
            P("wide", None),
            P("wide", None),
            P(("red", "tok"), "wide", None),
            P(("red", "tok"), "wide"),
            P("wide", None, ("red", "tok")),
            P("wide", ("red", "tok")),
        ),
        out_specs=P(("grp", "tok"), ("red", "wide")),
        check_vma=False,
    )
```

time: 255 us -> 234 us (0.918)
  waiting for transfers between devices: 109 us -> 39.7 us
  Pallas kernels: 0 us -> 49 us
  matrix products: 42.8 us -> 2.53 us
  local copies, waits for them, and re-layouts: 3.33 us -> 39.1 us
  blocking collectives: 51.7 us -> 40.5 us
  starting transfers between devices: 13.3 us -> 20 us
  other arithmetic: 20.5 us -> 25.2 us
  between operations: 14 us -> 16.9 us
    pallas_call x0 -> x13, Pallas kernels: none -> 49 us  [the longest x6 25 us: project_hidden(): pl.pallas_call(functools.partial(output_kernel, len(added), len(earlier))...]
    ppermute x8 -> x9, waiting for transfers between devices: 61.7 us -> 21.3 us  [sum_red(): total = total + lax.ppermute(x, 'red', pairs).astype(jnp.float32)]
    dot_general x12 -> x3, matrix products: 42.1 us -> 1.79 us  [body(): added = [jnp.dot(both, attn_rows, preferred_element_type=jnp.float32)]]
    reduce_scatter x2, waiting for transfers between devices: 44.2 us -> 5.93 us  [body(): summed = lax.psum_scatter(terms, 'wide', scatter_dimension=1, tiled=True)]
    unnamed x25 -> x62, local copies, waits for them, and re-layouts: 0.37 us -> 33.3 us
    all_gather x3 -> x2, blocking collectives: 51.7 us -> 40.5 us  [the longest x1 20.8 us: body(): lead = lax.all_gather(lead, 'wide', axis=1, tiled=True)]
    ppermute x0 -> x3, waiting for transfers between devices: none -> 4.64 us  [collect(): got = lax.ppermute(sent, 'wide', [(i, i ^ k) for i in range(n_wide)])]
    ppermute x15 -> x19, waiting for transfers between devices: 3.09 us -> 7.73 us  [swap(): return lax.ppermute(x, 'tok', [(0, 1), (1, 0)])]
  transfers between devices with their start and end apart: 25 -> 33, of which waited for: 11 -> 15; matrix products, arithmetic and copies ran while one was open for 24% -> 10% of each run, Pallas kernels for 0% -> 18%
where the time goes in v3:
time: 234 us; the launch traced here: 233 us
  Pallas kernels  49 us (21%)
  blocking collectives  40.5 us (17%)
  waiting for transfers between devices  39.7 us (17%)
  local copies, waits for them, and re-layouts  39.1 us (17%)
  other arithmetic  25.2 us (11%)
  starting transfers between devices  20 us (9%)
  between operations  16.9 us (7%)
  matrix products  2.53 us (1%)
    unnamed x62, local copies, waits for them, and re-layouts  33.3 us
    pallas_call x6, Pallas kernels, project_hidden(): pl.pallas_call(functools.partial(output_kernel, len(added), len(earlier))...  25 us
    pallas_call x7, Pallas kernels, project_tokens(): pl.pallas_call(functools.partial(project_kernel, len(earlier)), grid=(ste...  24 us
    ppermute x9, waiting for transfers between devices, sum_red(): total = total + lax.ppermute(x, 'red', pairs).astype(jnp.float32)  21.3 us
    all_gather x1, blocking collectives, body(): lead = lax.all_gather(lead, 'wide', axis=1, tiled=True)  20.8 us
    all_gather x1, blocking collectives, body(): rest = lax.all_gather(rest, 'wide', axis=1, tiled=True)  19.7 us
    convert_element_type x6, other arithmetic, body(): hidden = jax.nn.gelu(ups[c][p], approximate=False).astype(jnp.bfloat16)  15.9 us
    ppermute x9, starting transfers between devices, sum_red(): total = total + lax.ppermute(x, 'red', pairs).astype(jnp.float32)  11.5 us
  transfers between devices with their start and end apart: 33, of which 15 were waited for; matrix products, arithmetic and copies ran while one was open for 10% of the time, Pallas kernels for 18%

profile of v3, /device:TPU:0, one launch (start us, length us, event | category | flops | bytes accessed | tf_op | source)
XLA Modules:
  0.0 232.8 jit_solution(17835131873438342550)
XLA Ops:
  8.2 20.8 %all_gather.6 = bf16[120,3072]{1,0:T(8,128)(2,1)S(1)} all-gather(bf16[120,768]{1,0:T(8,128)(2,1)S(1)} %pad_maximum_fusion.5), channel_id=1, replica_groups=mesh['grp'=2,'wide'=4,'red'=2,'tok'=2] {'wide'}, dimensions={1}, use_global_device_ids=true | all-gather | bytes 921600 | tf_op jit(solution)/shard_map/all_gather | solution.py:184
  35.0 6.4 %copy-done.3 = bf16[1536,6144]{1,0:T(8,128)(2,1)S(1)} copy-done((bf16[1536,6144]{1,0:T(8,128)(2,1)S(1)}, bf16[1536,6144]{1,0:T(8,128)(2,1)}, u32[]{:S(2)}) %copy-start.3) | copy-done | bytes 18874392
  41.4 5.4 %shard_map.83 = (f32[112,4096]{1,0:T(8,128)S(1)}, bf16[112,4096]{1,0:T(8,128)(2,1)S(1)}) custom-call(bf16[112,1536]{1,0:T(8,128)(2,1)S(1)} %get-tuple-element.50.own_ref, bf16[112,1536]{1,0:T(8,128)(2,1)S(1)} %collective-permute-done.1.other_ref, bf16[1536,6144]{1,0:T(8,128)(2,1)S(1)} %copy-done.3), custom_call_target="tpu_custom_call" | custom-call | tf_op jit(solution)/shard_map/pallas_call | solution.py:85
  53.3 19.7 %all_gather.7 = bf16[144,3072]{1,0:T(8,128)(2,1)S(1)} all-gather(bf16[144,768]{1,0:T(8,128)(2,1)S(1)} %slice_add_fusion), channel_id=1, replica_groups=mesh['grp'=2,'wide'=4,'red'=2,'tok'=2] {'wide'}, dimensions={1}, use_global_device_ids=true | all-gather | bytes 1105920 | tf_op jit(solution)/shard_map/all_gather | solution.py:202
  73.0 4.8 %fusion.2 = (bf16[112,4096]{1,0:T(8,128)(2,1)}, f32[112,4096]{1,0:T(8,128)S(1)}) fusion(bf16[112,4096]{1,0:T(8,128)(2,1)S(1)} %collective-permute-done.5, bf16[112,4096]{1,0:T(8,128)(2,1)S(1)} %add_convert_fusion.refs_0_), kind=kLoop, calls=%fused_computation.7 | loop fusion | flops 31195136 | bytes 4587520 | tf_op jit(solution)/shard_map/convert_element_type | solution.py:229
  86.8 3.0 %shard_map.84 = (f32[80,2048]{1,0:T(8,128)S(1)}, bf16[80,2048]{1,0:T(8,128)(2,1)}) custom-call(bf16[80,1536]{1,0:T(8,128)(2,1)S(1)} %constant_dynamic-slice_fusion.own_ref, bf16[80,1536]{1,0:T(8,128)(2,1)S(1)} %slice.157.other_ref, bf16[1536,6144]{1,0:T(8,128)(2,1)S(1)} %bitcast.41, bf16[112,2048]{1,0:T(8,128)(2,1)S(1)} %add_convert_fusion.3.refs_0_), custom_call_target="tpu_custom_call" | custom-call | tf_op jit(solution)/shard_map/pallas_call | solution.py:85
  92.5 6.4 %copy-done.4 = bf16[1536,6144]{1,0:T(8,128)(2,1)S(1)} copy-done((bf16[1536,6144]{1,0:T(8,128)(2,1)S(1)}, bf16[1536,6144]{1,0:T(8,128)(2,1)}, u32[]{:S(2)}) %copy-start.4) | copy-done | bytes 18874392
  98.9 4.6 %shard_map.89 = (f32[80,4096]{1,0:T(8,128)S(1)}, bf16[80,4096]{1,0:T(8,128)(2,1)S(1)}) custom-call(bf16[80,1536]{1,0:T(8,128)(2,1)S(1)} %constant_dynamic-slice_fusion.own_ref, bf16[80,1536]{1,0:T(8,128)(2,1)S(1)} %slice.157.other_ref, bf16[1536,6144]{1,0:T(8,128)(2,1)S(1)} %copy-done.4, bf16[112,4096]{1,0:T(8,128)(2,1)S(1)} %add_convert_fusion.refs_0_), custom_call_target="tpu_custom_call" | custom-call | tf_op jit(solution)/shard_map/pallas_call | solution.py:85
  119.1 7.0 %shard_map.86.refs_0_ = f32[224,1536]{1,0:T(8,128)S(1)} custom-call(bf16[112,4096]{1,0:T(8,128)(2,1)} %get-tuple-element.41.own_ref, bf16[112,4096]{1,0:T(8,128)(2,1)S(1)} %collective-permute-done.11.other_ref, bf16[6144,1536]{1,0:T(8,128)(2,1)S(1)} %bitcast.39), custom_call_target="tpu_custom_call" | custom-call | tf_op jit(solution)/shard_map/pallas_call | solution.py:132
  128.1 3.1 %fusion.38.own_ref = bf16[112,2048]{1,0:T(8,128)(2,1)S(1)} fusion(bf16[112,2048]{1,0:T(8,128)(2,1)} %collective-permute-done.3, bf16[112,2048]{1,0:T(8,128)(2,1)S(1)} %add_convert_fusion.3.refs_0_, f32[]{:T(128)} %bitcast.11), kind=kLoop, calls=%fused_computation.81 | loop fusion | flops 15826944 | bytes 1376260 | tf_op jit(solution)/shard_map/convert_element_type | solution.py:229
  131.6 6.4 %copy-done.5 = bf16[1536,6144]{1,0:T(8,128)(2,1)S(1)} copy-done((bf16[1536,6144]{1,0:T(8,128)(2,1)S(1)}, bf16[1536,6144]{1,0:T(8,128)(2,1)}, u32[]{:S(2)}) %copy-start.5) | copy-done | bytes 18874392
  137.9 5.1 %shard_map.92 = (f32[64,4096]{1,0:T(8,128)S(1)}, bf16[64,4096]{1,0:T(8,128)(2,1)}) custom-call(bf16[64,1536]{1,0:T(8,128)(2,1)S(1)} %dynamic-slice.own_ref, bf16[64,1536]{1,0:T(8,128)(2,1)S(1)} %slice.156.other_ref, bf16[1536,6144]{1,0:T(8,128)(2,1)S(1)} %copy-done.5, bf16[80,4096]{1,0:T(8,128)(2,1)S(1)} %add_convert_fusion.1.refs_0_), custom_call_target="tpu_custom_call" | custom-call | tf_op jit(solution)/shard_map/pallas_call | solution.py:85
  147.8 2.9 %shard_map.88 = bf16[224,1536]{1,0:T(8,128)(2,1)S(1)} custom-call(bf16[112,2048]{1,0:T(8,128)(2,1)S(1)} %fusion.38.own_ref, bf16[112,2048]{1,0:T(8,128)(2,1)S(1)} %collective-permute-done.10.other_ref, bf16[6144,1536]{1,0:T(8,128)(2,1)S(1)} %bitcast.39, f32[224,1536]{1,0:T(8,128)S(1)} %copy-done.7, f32[224,1536]{1,0:T(8,128)S(1)} %fusion.70.refs_1_), custom_call_target="tpu_custom_call" | custom-call | tf_op jit(solution)/shard_map/pallas_call | solution.py:132
  151.2 8.9 %collective-permute-done.19 = bf16[80,4096]{1,0:T(8,128)(2,1)S(1)} collective-permute-done((bf16[80,4096]{1,0:T(8,128)(2,1)S(1)}, bf16[80,4096]{1,0:T(8,128)(2,1)S(1)}, u32[]{:S(2)}, u32[]{:S(2)}) %collective-permute-start.19) | collective-permute-done | bytes 655392 | tf_op jit(solution)/shard_map/ppermute | solution.py:160
  160.1 2.9 %fusion.17.own_ref = bf16[80,4096]{1,0:T(8,128)(2,1)S(1)} fusion(bf16[80,4096]{1,0:T(8,128)(2,1)S(1)} %collective-permute-done.19, bf16[80,4096]{1,0:T(8,128)(2,1)S(1)} %add_convert_fusion.1.refs_0_), kind=kLoop, calls=%fused_computation.37 | loop fusion | flops 22282240 | bytes 1966080 | tf_op jit(solution)/shard_map/convert_element_type | solution.py:229
  165.2 6.5 %copy-done.1 = bf16[6144,1536]{1,0:T(8,128)(2,1)S(1)} copy-done((bf16[6144,1536]{1,0:T(8,128)(2,1)S(1)}, bf16[6144,1536]{1,0:T(8,128)(2,1)}, u32[]{:S(2)}) %copy-start.1) | copy-done | bytes 18874392
  171.7 4.4 %shard_map.90.refs_0_ = f32[160,1536]{1,0:T(8,128)S(1)} custom-call(bf16[80,4096]{1,0:T(8,128)(2,1)S(1)} %fusion.17.own_ref, bf16[80,4096]{1,0:T(8,128)(2,1)S(1)} %collective-permute-done.20.other_ref, bf16[6144,1536]{1,0:T(8,128)(2,1)S(1)} %copy-done.1), custom_call_target="tpu_custom_call" | custom-call | tf_op jit(solution)/shard_map/pallas_call | solution.py:132
  176.2 3.6 %shard_map.91 = bf16[160,1536]{1,0:T(8,128)(2,1)S(1)} custom-call(bf16[80,2048]{1,0:T(8,128)(2,1)S(1)} %fusion.48.own_ref, bf16[80,2048]{1,0:T(8,128)(2,1)} %collective-permute-done.17.other_ref, bf16[6144,1536]{1,0:T(8,128)(2,1)S(1)} %copy-done.1, f32[160,1536]{1,0:T(8,128)S(1)} %shard_map.90.refs_0_, f32[160,1536]{1,0:T(8,128)S(1)} %copy-done.8), custom_call_target="tpu_custom_call" | custom-call | tf_op jit(solution)/shard_map/pallas_call | solution.py:132
  181.6 5.0 %reduce-scatter.3.cloned.1.call-done = bf16[112,768]{1,0:T(8,128)(2,1)} async-done(((bf16[112,3072]{1,0:T(8,128)(2,1)}), bf16[112,768]{1,0:T(8,128)(2,1)}) %reduce-scatter.3.cloned.1.call-update) | async-done | bytes 172048 | tf_op jit(solution)/shard_map/reduce_scatter | solution.py:245
  188.7 5.6 %collective-permute-done.25 = bf16[64,4096]{1,0:T(8,128)(2,1)S(1)} collective-permute-done((bf16[64,4096]{1,0:T(8,128)(2,1)S(1)}, bf16[64,4096]{1,0:T(8,128)(2,1)S(1)}, u32[]{:S(2)}, u32[]{:S(2)}) %collective-permute-start.25) | collective-permute-done | bytes 524320 | tf_op jit(solution)/shard_map/ppermute | solution.py:160
  198.8 6.5 %copy-done.2 = bf16[6144,1536]{1,0:T(8,128)(2,1)S(1)} copy-done((bf16[6144,1536]{1,0:T(8,128)(2,1)S(1)}, bf16[6144,1536]{1,0:T(8,128)(2,1)}, u32[]{:S(2)}) %copy-start.2) | copy-done | bytes 18874392
  205.2 3.9 %shard_map.93.refs_0_ = f32[128,1536]{1,0:T(8,128)S(1)} custom-call(bf16[64,4096]{1,0:T(8,128)(2,1)S(1)} %fusion.28.own_ref, bf16[64,4096]{1,0:T(8,128)(2,1)S(1)} %collective-permute-done.26.other_ref, bf16[6144,1536]{1,0:T(8,128)(2,1)S(1)} %copy-done.2), custom_call_target="tpu_custom_call" | custom-call | tf_op jit(solution)/shard_map/pallas_call | solution.py:132
  209.1 3.2 %shard_map.94 = bf16[128,1536]{1,0:T(8,128)(2,1)S(1)} custom-call(bf16[64,2048]{1,0:T(8,128)(2,1)S(1)} %fusion.58.own_ref, bf16[64,2048]{1,0:T(8,128)(2,1)} %collective-permute-done.23.other_ref, bf16[6144,1536]{1,0:T(8,128)(2,1)S(1)} %copy-done.2, f32[128,1536]{1,0:T(8,128)S(1)} %shard_map.93.refs_0_, f32[128,1536]{1,0:T(8,128)S(1)} %fusion.66.refs_1_), custom_call_target="tpu_custom_call" | custom-call | tf_op jit(solution)/shard_map/pallas_call | solution.py:132
  220.8 4.1 %collective-permute-done.29 = bf16[64,768]{1,0:T(8,128)(2,1)S(1)} collective-permute-done((bf16[64,768]{1,0:T(8,128)(2,1)S(1)}, bf16[64,768]{1,0:T(8,128)(2,1)S(1)}, u32[]{:S(2)}, u32[]{:S(2)}) %collective-permute-start.29) | collective-permute-done | bytes 98336 | tf_op jit(solution)/shard_map/ppermute | solution.py:168
  (194 shorter events, 65.8 us)
Async XLA Ops:
  6.5 180.1 %reduce-scatter.3.cloned.1.call-start = ((), (), s32[]{:S(2)}) async-start(), calls=%async_computation.2 | async-start | bytes 860160 | tf_op jit(solution)/shard_map/reduce_scatter | solution.py:245
  29.3 3.6 %collective-permute-start = (f32[2,112]{1,0:T(2,128)S(1)}, f32[2,112]{1,0:T(2,128)S(1)}, u32[]{:S(2)}, u32[]{:S(2)}) collective-permute-start(f32[2,112]{1,0:T(2,128)S(1)} %pad_maximum_fusion.7), channel_id=1, source_target_pairs={{0,2},{2,0},{1,3},{3,1},{4,6},{6,4},{5,7},{7,5},{8,10},{10,8},{9,1... | collective-permute-start | bytes 2696 | tf_op jit(solution)/shard_map/ppermute | solution.py:160
  50.4 22.6 %collective-permute-start.5 = (bf16[112,4096]{1,0:T(8,128)(2,1)S(1)}, bf16[112,4096]{1,0:T(8,128)(2,1)S(1)}, u32[]{:S(2)}, u32[]{:S(2)}) collective-permute-start(bf16[112,4096]{1,0:T(8,128)(2,1)S(1)} %add_convert_fusion.refs_0_), channel_id=1, source_target_pairs={{0,2},{2,0},{1,3},{3,1},{4,6},{6,4},{5,7},{7,5},{8,10},{10,8},{9,1... | collective-permute-start | bytes 2752520 | tf_op jit(solution)/shard_map/ppermute | solution.py:160
  79.4 3.6 %collective-permute-start.6 = (f32[2,144]{1,0:T(2,128)S(1)}, f32[2,144]{1,0:T(2,128)S(1)}, u32[]{:S(2)}, u32[]{:S(2)}) collective-permute-start(f32[2,144]{1,0:T(2,128)S(1)} %pad_maximum_fusion.6), channel_id=1, source_target_pairs={{0,2},{2,0},{1,3},{3,1},{4,6},{6,4},{5,7},{7,5},{8,10},{10,8},{9,1... | collective-permute-start | bytes 3464 | tf_op jit(solution)/shard_map/ppermute | solution.py:160
  86.5 19.5 %collective-permute-start.12 = (bf16[256,384]{1,0:T(8,128)(2,1)S(1)}, bf16[256,384]{1,0:T(8,128)(2,1)}, u32[]{:S(2)}, u32[]{:S(2)}) collective-permute-start(bf16[256,384]{1,0:T(8,128)(2,1)S(1)} %get-tuple-element.28), channel_id=1, source_target_pairs={{0,1},{1,0},{2,3},{3,2},{4,5},{5,4},{6,7},{7,6},{8,9},{9,8},{10,11... | collective-permute-start | bytes 589832 | tf_op jit(solution)/shard_map/ppermute | solution.py:154
  89.9 17.9 %collective-permute-start.8 = (bf16[80,2048]{1,0:T(8,128)(2,1)}, bf16[80,2048]{1,0:T(8,128)(2,1)}, u32[]{:S(2)}, u32[]{:S(2)}) collective-permute-start(bf16[80,2048]{1,0:T(8,128)(2,1)} %get-tuple-element.24), channel_id=1, source_target_pairs={{0,1},{1,0},{2,3},{3,2},{4,5},{5,4},{6,7},{7,6},{8,9},{9,8},{10,11... | collective-permute-start | bytes 983048 | tf_op jit(solution)/shard_map/ppermute | solution.py:154
  90.2 37.9 %collective-permute-start.3 = (bf16[112,2048]{1,0:T(8,128)(2,1)S(1)}, bf16[112,2048]{1,0:T(8,128)(2,1)}, u32[]{:S(2)}, u32[]{:S(2)}) collective-permute-start(bf16[112,2048]{1,0:T(8,128)(2,1)S(1)} %add_convert_fusion.3.refs_0_), channel_id=1, source_target_pairs={{0,2},{2,0},{1,3},{3,1},{4,6},{6,4},{5,7},{7,5},{8,10},{10,8},{9,1... | collective-permute-start | bytes 1376264 | tf_op jit(solution)/shard_map/ppermute | solution.py:160
  91.6 27.5 %collective-permute-start.11 = (bf16[112,4096]{1,0:T(8,128)(2,1)}, bf16[112,4096]{1,0:T(8,128)(2,1)S(1)}, u32[]{:S(2)}, u32[]{:S(2)}) collective-permute-start(bf16[112,4096]{1,0:T(8,128)(2,1)} %get-tuple-element.41.own_ref), channel_id=1, source_target_pairs={{0,1},{1,0},{2,3},{3,2},{4,5},{5,4},{6,7},{7,6},{8,9},{9,8},{10,11... | collective-permute-start | bytes 2752520 | tf_op jit(solution)/shard_map/ppermute | solution.py:154
  104.6 26.8 %collective-permute-start.18 = (bf16[80,4096]{1,0:T(8,128)(2,1)S(1)}, bf16[80,4096]{1,0:T(8,128)(2,1)S(1)}, u32[]{:S(2)}, u32[]{:S(2)}) collective-permute-start(bf16[80,4096]{1,0:T(8,128)(2,1)S(1)} %get-tuple-element.30), channel_id=1, source_target_pairs={{0,1},{1,0},{2,3},{3,2},{4,5},{5,4},{6,7},{7,6},{8,9},{9,8},{10,11... | collective-permute-start | bytes 1966088 | tf_op jit(solution)/shard_map/ppermute | solution.py:154
  107.0 7.8 %collective-permute-start.13 = (bf16[256,384]{1,0:T(8,128)(2,1)S(1)}, bf16[256,384]{1,0:T(8,128)(2,1)S(1)}, u32[]{:S(2)}, u32[]{:S(2)}) collective-permute-start(bf16[256,384]{1,0:T(8,128)(2,1)S(1)} %add_convert_fusion.6), channel_id=1, source_target_pairs={{0,2},{2,0},{1,3},{3,1},{4,6},{6,4},{5,7},{7,5},{8,10},{10,8},{9,1... | collective-permute-start | bytes 589832 | tf_op jit(solution)/shard_map/ppermute | solution.py:160
  108.9 35.7 %collective-permute-start.16 = (bf16[80,2048]{1,0:T(8,128)(2,1)S(1)}, bf16[80,2048]{1,0:T(8,128)(2,1)S(1)}, u32[]{:S(2)}, u32[]{:S(2)}) collective-permute-start(bf16[80,2048]{1,0:T(8,128)(2,1)S(1)} %add_convert_fusion.4.refs_0_), channel_id=1, source_target_pairs={{0,2},{2,0},{1,3},{3,1},{4,6},{6,4},{5,7},{7,5},{8,10},{10,8},{9,1... | collective-permute-start | bytes 983048 | tf_op jit(solution)/shard_map/ppermute | solution.py:160
  117.3 8.8 %collective-permute-start.9 = (bf16[64,2048]{1,0:T(8,128)(2,1)S(1)}, bf16[64,2048]{1,0:T(8,128)(2,1)S(1)}, u32[]{:S(2)}, u32[]{:S(2)}) collective-permute-start(bf16[64,2048]{1,0:T(8,128)(2,1)S(1)} %get-tuple-element.26), channel_id=1, source_target_pairs={{0,1},{1,0},{2,3},{3,2},{4,5},{5,4},{6,7},{7,6},{8,9},{9,8},{10,11... | collective-permute-start | bytes 786440 | tf_op jit(solution)/shard_map/ppermute | solution.py:154
  126.2 20.2 %collective-permute-start.22 = (bf16[64,2048]{1,0:T(8,128)(2,1)S(1)}, bf16[64,2048]{1,0:T(8,128)(2,1)S(1)}, u32[]{:S(2)}, u32[]{:S(2)}) collective-permute-start(bf16[64,2048]{1,0:T(8,128)(2,1)S(1)} %add_convert_fusion.5), channel_id=1, source_target_pairs={{0,2},{2,0},{1,3},{3,1},{4,6},{6,4},{5,7},{7,5},{8,10},{10,8},{9,1... | collective-permute-start | bytes 786440 | tf_op jit(solution)/shard_map/ppermute | solution.py:160
  131.2 16.6 %collective-permute-start.10 = (bf16[112,2048]{1,0:T(8,128)(2,1)S(1)}, bf16[112,2048]{1,0:T(8,128)(2,1)S(1)}, u32[]{:S(2)}, u32[]{:S(2)}) collective-permute-start(bf16[112,2048]{1,0:T(8,128)(2,1)S(1)} %fusion.38.own_ref), channel_id=1, source_target_pairs={{0,1},{1,0},{2,3},{3,2},{4,5},{5,4},{6,7},{7,6},{8,9},{9,8},{10,11... | collective-permute-start | bytes 1376264 | tf_op jit(solution)/shard_map/ppermute | solution.py:154
  143.0 17.1 %collective-permute-start.19 = (bf16[80,4096]{1,0:T(8,128)(2,1)S(1)}, bf16[80,4096]{1,0:T(8,128)(2,1)S(1)}, u32[]{:S(2)}, u32[]{:S(2)}) collective-permute-start(bf16[80,4096]{1,0:T(8,128)(2,1)S(1)} %add_convert_fusion.1.refs_0_), channel_id=1, source_target_pairs={{0,2},{2,0},{1,3},{3,1},{4,6},{6,4},{5,7},{7,5},{8,10},{10,8},{9,1... | collective-permute-start | bytes 1966088 | tf_op jit(solution)/shard_map/ppermute | solution.py:160
  144.4 35.6 %collective-permute-start.24 = (bf16[64,4096]{1,0:T(8,128)(2,1)}, bf16[64,4096]{1,0:T(8,128)(2,1)S(1)}, u32[]{:S(2)}, u32[]{:S(2)}) collective-permute-start(bf16[64,4096]{1,0:T(8,128)(2,1)} %get-tuple-element.32), channel_id=1, source_target_pairs={{0,1},{1,0},{2,3},{3,2},{4,5},{5,4},{6,7},{7,6},{8,9},{9,8},{10,11... | collective-permute-start | bytes 1572872 | tf_op jit(solution)/shard_map/ppermute | solution.py:154
  146.0 30.2 %collective-permute-start.17 = (bf16[80,2048]{1,0:T(8,128)(2,1)S(1)}, bf16[80,2048]{1,0:T(8,128)(2,1)}, u32[]{:S(2)}, u32[]{:S(2)}) collective-permute-start(bf16[80,2048]{1,0:T(8,128)(2,1)S(1)} %fusion.48.own_ref), channel_id=1, source_target_pairs={{0,1},{1,0},{2,3},{3,2},{4,5},{5,4},{6,7},{7,6},{8,9},{9,8},{10,11... | collective-permute-start | bytes 983048 | tf_op jit(solution)/shard_map/ppermute | solution.py:154
  147.6 61.5 %collective-permute-start.23 = (bf16[64,2048]{1,0:T(8,128)(2,1)S(1)}, bf16[64,2048]{1,0:T(8,128)(2,1)}, u32[]{:S(2)}, u32[]{:S(2)}) collective-permute-start(bf16[64,2048]{1,0:T(8,128)(2,1)S(1)} %fusion.58.own_ref), channel_id=1, source_target_pairs={{0,1},{1,0},{2,3},{3,2},{4,5},{5,4},{6,7},{7,6},{8,9},{9,8},{10,11... | collective-permute-start | bytes 786440 | tf_op jit(solution)/shard_map/ppermute | solution.py:154
  150.8 12.4 %collective-permute-start.15 = (bf16[112,1536]{1,0:T(8,128)(2,1)S(1)}, bf16[112,1536]{1,0:T(8,128)(2,1)S(1)}, u32[]{:S(2)}, u32[]{:S(2)}) collective-permute-start(bf16[112,1536]{1,0:T(8,128)(2,1)S(1)} %slice.165), channel_id=1, source_target_pairs={{0,1},{1,0},{2,3},{3,2},{4,5},{5,4},{6,7},{7,6},{8,9},{9,8},{10,11... | collective-permute-start | bytes 1032200 | tf_op jit(solution)/shard_map/ppermute | solution.py:154
  164.1 55.3 %reduce-scatter.5.cloned.1.call-start = ((), (), s32[]{:S(2)}) async-start(), calls=%async_computation.3 | async-start | bytes 614400 | tf_op jit(solution)/shard_map/reduce_scatter | solution.py:245
  180.1 14.3 %collective-permute-start.25 = (bf16[64,4096]{1,0:T(8,128)(2,1)S(1)}, bf16[64,4096]{1,0:T(8,128)(2,1)S(1)}, u32[]{:S(2)}, u32[]{:S(2)}) collective-permute-start(bf16[64,4096]{1,0:T(8,128)(2,1)S(1)} %add_convert_fusion.2), channel_id=1, source_target_pairs={{0,2},{2,0},{1,3},{3,1},{4,6},{6,4},{5,7},{7,5},{8,10},{10,8},{9,1... | collective-permute-start | bytes 1572872 | tf_op jit(solution)/shard_map/ppermute | solution.py:160
  214.0 6.8 %collective-permute-start.30 = (bf16[64,768]{1,0:T(8,128)(2,1)S(1)}, bf16[64,768]{1,0:T(8,128)(2,1)S(1)}, u32[]{:S(2)}, u32[]{:S(2)}) collective-permute-start(bf16[64,768]{1,0:T(8,128)(2,1)S(1)} %get-tuple-element.55), channel_id=1, source_target_pairs={{0,4},{4,0},{8,12},{12,8},{1,5},{5,1},{9,13},{13,9},{2,6},{6,2},{1... | collective-permute-start | bytes 294920 | tf_op jit(solution)/shard_map/ppermute | solution.py:168
  214.1 10.9 %collective-permute-start.29 = (bf16[64,768]{1,0:T(8,128)(2,1)S(1)}, bf16[64,768]{1,0:T(8,128)(2,1)S(1)}, u32[]{:S(2)}, u32[]{:S(2)}) collective-permute-start(bf16[64,768]{1,0:T(8,128)(2,1)S(1)} %get-tuple-element.54), channel_id=1, source_target_pairs={{0,8},{4,12},{8,0},{12,4},{1,9},{5,13},{9,1},{13,5},{2,10},{6,14},... | collective-permute-start | bytes 294920 | tf_op jit(solution)/shard_map/ppermute | solution.py:168
  216.4 8.6 %collective-permute-start.28 = (bf16[64,768]{1,0:T(8,128)(2,1)S(1)}, bf16[64,768]{1,0:T(8,128)(2,1)S(1)}, u32[]{:S(2)}, u32[]{:S(2)}) collective-permute-start(bf16[64,768]{1,0:T(8,128)(2,1)S(1)} %get-tuple-element.53), channel_id=1, source_target_pairs={{0,12},{4,8},{8,4},{12,0},{1,13},{5,9},{9,5},{13,1},{2,14},{6,10},... | collective-permute-start | bytes 294920 | tf_op jit(solution)/shard_map/ppermute | solution.py:168
  (41 other events, 468.5 us)
Sparse Core Ops, SparseCore 0:
  164.2 22.3 reduce-scatter.2
  197.8 21.5 reduce-scatter.4
